TPU v7x, 32 devices: a whole 2x2x4 slice. The times are simulated.
32 devices in a mesh: dp: 16 (over z, y, x), mp: 2 (over core).
Axes of the slice: x: 2, y: 2, z: 4, core: 2. Of those that a mesh axis runs over, the one named last changes fastest.
Arguments:
- source: bfloat16 [256, 8, 512], P('dp'), may hold values from -6 to 6
- target: bfloat16 [256, 8, 512], P('dp'), may hold values from -6 to 6
- lengths: int32 [256, 2], P('dp'), may hold values from 1 to 8, as said below
- destinations: int32 [256], P('dp'), may hold values from 0 to 15, as said below
- cotangent: bfloat16 [256, 8, 512], P('dp'), may hold values from -6 to 6
- square_master: float32 [12, 512, 512], P(None, 'dp', 'mp'), may hold values from -2 to 2
- wide_master: float32 [4, 512, 2048], P(None, 'dp', 'mp'), may hold values from -2 to 2
- norm_master: float32 [10, 512], P(None, 'dp'), may hold values from -2 to 4
- square_rows: float32 [12, 512], P(None, 'dp'), may hold values from 61.44 to 245.76
- square_cols: float32 [12, 512], P(None, 'mp'), may hold values from 61.44 to 245.76
- wide_rows: float32 [4, 512], P(None, 'dp'), may hold values from 102.4 to 409.6
- wide_cols: float32 [4, 2048], P(None, 'mp'), may hold values from 102.4 to 409.6
- gain_offset_moment: float32 [10, 512], P(None, 'dp'), may hold values from 307.2 to 1228.8
Outputs:
- decoded: bfloat16 [256, 8, 512], P('dp', 'mp')
- source_grad: float32 [256, 8, 512], P('dp', 'mp')
- target_grad: float32 [256, 8, 512], P('dp')
- square_grad: float32 [12, 512, 512], P(None, 'dp', 'mp')
- square_rows_new: float32 [12, 512], P(None, 'dp')
- square_cols_new: float32 [12, 512], P(None, 'mp')
- updated_square_masters: float32 [12, 512, 512], P(None, 'dp', 'mp')
- square_copy: bfloat16 [12, 512, 512], P(None, 'dp', 'mp')
- wide_grad: float32 [4, 512, 2048], P(None, 'dp', 'mp')
- wide_rows_new: float32 [4, 512], P(None, 'dp')
- wide_cols_new: float32 [4, 2048], P(None, 'mp')
- wide_new: float32 [4, 512, 2048], P(None, 'dp', 'mp')
- wide_copy: bfloat16 [4, 512, 2048], P(None, 'dp', 'mp')
- norm_grad: float32 [10, 512], P(None, 'dp')
- norm_second_new: float32 [10, 512], P(None, 'dp')
- norm_new: float32 [10, 512], P(None, 'dp')
- norm_copy: bfloat16 [10, 512], P(None, 'dp')
Inputs may be any that keep to these rules, and one draw needn't show every extreme that they name: Column 0 holds source lengths and column 1 target lengths; each column holds 8 at least once. `destinations`: among the 16 pairs of each device, every device is named exactly 1 times.
All inputs are finite; a program needn't handle non-finite values.
Results may differ from a plain program's by a relative error of at most 0.02.
The roundings to bfloat16 on the way count: a program that leaves them out, or rounds other values in their place, can miss the bound.
Values may be sent and summed in bfloat16 or wider, within the bound.
A program may use at most 192 MiB of HBM per device.

v0:
```python
import jax
import jax.numpy as jnp
from jax import lax
from jax.sharding import PartitionSpec as P

FF = 2048
HEADS = 8
MICRO = 2


RATE = 0.03
NORM_RATE = 0.2


def rounded(input_tensor):
    return input_tensor.astype(jnp.bfloat16)


def identity(input_tensor):
    return input_tensor


def project(input_tensor, weight_matrix):
    return jnp.einsum(
        "rft,tv->rfv", input_tensor, weight_matrix, preferred_element_type=jnp.float32
    )


def project_back(input_tensor, weight_matrix):
    return jnp.einsum(
        "cxk,ak->cxa", input_tensor, weight_matrix, preferred_element_type=jnp.float32
    )


def outer_sum(first_factor_array, second_factor_array):
    return jnp.einsum(
        "zmb,zmf->bf", first_factor_array, second_factor_array, preferred_element_type=jnp.float32
    )


def split_heads(input_tensor, head_size):
    return input_tensor.reshape(
        input_tensor.shape[0], input_tensor.shape[1], input_tensor.shape[2] // head_size, head_size
    )


def merge_heads(input_tensor):
    return input_tensor.reshape(
        input_tensor.shape[0], input_tensor.shape[1], input_tensor.shape[2] * input_tensor.shape[3]
    )


def layer_norm(residual, gain_row, bias_row):
    centred = residual - jnp.mean(residual, axis=-1, keepdims=True)
    spread = lax.rsqrt(jnp.mean(centred * centred, axis=-1, keepdims=True) + 1e-05)
    normed = centred * spread
    return (normed * gain_row + bias_row, (normed, spread))


def norm_back(upstream, gain_row, kept_state, pick):
    normed, spread = kept_state
    scaled = upstream * gain_row
    centred_grad = (
        scaled
        - jnp.mean(scaled, axis=-1, keepdims=True)
        - normed * jnp.mean(scaled * normed, axis=-1, keepdims=True)
    )
    return (
        centred_grad * spread,
        jnp.sum(pick(upstream * normed), axis=(0, 1)),
        jnp.sum(pick(upstream), axis=(0, 1)),
    )


def attend_forward(query_in, key_in, matrices, start_index, allowed, head_size):
    queries = split_heads(rounded(project(query_in, matrices[start_index])), head_size)
    key_rows = split_heads(rounded(project(key_in, matrices[start_index + 1])), head_size)
    content_lines = split_heads(rounded(project(key_in, matrices[start_index + 2])), head_size)
    scores = jnp.einsum(
        "sqhe,skhe->shqk", queries, key_rows, preferred_element_type=jnp.float32
    ) * head_size ** (-0.5)
    scores = jnp.where(allowed[:, None], scores, -1000000000.0)
    attn_probs = jax.nn.softmax(scores, axis=-1)
    probs_low = rounded(attn_probs)
    mixed_heads = rounded(
        merge_heads(
            jnp.einsum(
                "shqk,skhe->sqhe", probs_low, content_lines, preferred_element_type=jnp.float32
            )
        )
    )
    partial_value = project_back(mixed_heads, matrices[start_index + 3])
    return (partial_value, (queries, key_rows, content_lines, attn_probs, probs_low, mixed_heads))


def attend_back(upstream, query_in, key_in, matrices, start_index, kept_state, head_size):
    queries, key_rows, content_lines, attn_probs, probs_low, mixed_heads = kept_state
    scale = head_size ** (-0.5)
    out_grad = outer_sum(upstream, mixed_heads)
    mixed_grad = split_heads(rounded(project(upstream, matrices[start_index + 3])), head_size)
    prob_grad = jnp.einsum(
        "sqhe,skhe->shqk", mixed_grad, content_lines, preferred_element_type=jnp.float32
    )
    value_grad = rounded(
        jnp.einsum("shqk,sqhe->skhe", probs_low, mixed_grad, preferred_element_type=jnp.float32)
    )
    score_grad = rounded(
        attn_probs * (prob_grad - jnp.sum(attn_probs * prob_grad, axis=-1, keepdims=True))
    )
    query_grad = rounded(
        jnp.einsum("shqk,skhe->sqhe", score_grad, key_rows, preferred_element_type=jnp.float32)
        * scale
    )
    key_grad = rounded(
        jnp.einsum("shqk,sqhe->skhe", score_grad, queries, preferred_element_type=jnp.float32)
        * scale
    )
    query_grad = merge_heads(query_grad)
    key_grad = merge_heads(key_grad)
    value_grad = merge_heads(value_grad)
    weight_grads = (
        outer_sum(query_in, query_grad),
        outer_sum(key_in, key_grad),
        outer_sum(key_in, value_grad),
        out_grad,
    )
    asking_piece = project_back(query_grad, matrices[start_index])
    key_part = project_back(key_grad, matrices[start_index + 1]) + project_back(
        value_grad, matrices[start_index + 2]
    )
    return (asking_piece, key_part, weight_grads)


def expand_forward(inputs, matrices, start_index):
    hidden = project(inputs, matrices[start_index])
    active = rounded(jax.nn.gelu(hidden))
    return (project_back(active, matrices[start_index + 1]), (hidden, active))


def expand_back(upstream, inputs, matrices, start_index, kept_state):
    hidden, active = kept_state
    down_grad = outer_sum(upstream, active)
    active_grad = rounded(project(upstream, matrices[start_index + 1]))
    unused, pullback = jax.vjp(jax.nn.gelu, hidden)
    hidden_grad = rounded(pullback(active_grad.astype(jnp.float32))[0])
    up_grad = outer_sum(inputs, hidden_grad)
    return (project_back(hidden_grad, matrices[start_index]), up_grad, down_grad)


def accumulate(totals, position, addend):
    totals[position] = addend if totals[position] is None else totals[position] + addend


def shards(
    source,
    target,
    lengths,
    destinations,
    cotangent,
    square_master,
    wide_master,
    norm_master,
    square_rows,
    square_cols,
    wide_rows,
    wide_cols,
    gain_offset_moment,
):
    peer_count = lax.axis_size("dp")
    sent_dev = source.shape[0]
    slot_count = source.shape[1]
    model_width = source.shape[2]
    per_peer = sent_dev // peer_count
    head_size = model_width // HEADS
    per_block = sent_dev // MICRO
    half_len = slot_count // lax.axis_size("mp")
    half_start = lax.axis_index("mp") * half_len
    send_order = jnp.argsort(destinations, stable=True)
    home_place = jnp.argsort(send_order, stable=True)

    def own_half(input_tensor):
        return lax.dynamic_slice_in_dim(input_tensor, half_start, half_len, 1)

    def share_total(partial_value):
        return lax.psum_scatter(partial_value, "mp", scatter_dimension=1, tiled=True)

    def add_branch(residual, partial_value):
        return residual + share_total(partial_value)

    def low_rows(value):
        return lax.all_gather(rounded(value), "mp", axis=1, tiled=True)

    def by_peer(input_tensor):
        return jnp.take(input_tensor, send_order, axis=0).reshape(
            (peer_count, per_peer) + input_tensor.shape[1:]
        )

    def flatten(input_tensor):
        return input_tensor.reshape((sent_dev,) + input_tensor.shape[2:])

    moved_lengths = flatten(
        lax.all_to_all(by_peer(lengths), "dp", split_axis=0, concat_axis=0, tiled=True)
    )
    square_low, wide_low, norm_low = (
        lax.all_gather(rounded(square_master), "dp", axis=1, tiled=True),
        lax.all_gather(rounded(wide_master), "dp", axis=1, tiled=True),
        lax.all_gather(rounded(norm_master), "dp", axis=1, tiled=True),
    )
    gain_rows = norm_low[:5].astype(jnp.float32)
    bias_rows = norm_low[5:].astype(jnp.float32)
    positions = jnp.arange(slot_count)
    causal = positions[None, :] <= positions[:, None]

    def key_mask(counts):
        return jnp.broadcast_to(
            positions[None, None, :] < counts[:, None, None],
            (counts.shape[0], slot_count, slot_count),
        )

    square_grads = [None] * 12
    wide_grads = [None] * 4
    gain_grads = [None] * 5
    bias_grads = [None] * 5

    def norm_step(upstream, position, kept_state):
        residual_grad, gain_grad, bias_grad = norm_back(
            upstream, gain_rows[position], kept_state, identity
        )
        accumulate(gain_grads, position, gain_grad)
        accumulate(bias_grads, position, bias_grad)
        return residual_grad

    def attend_step(upstream_low, query_in, key_in, start_index, kept_state):
        asking_piece, key_part, weight_grads = attend_back(
            upstream_low, query_in, key_in, square_low, start_index, kept_state, head_size
        )
        for offset in range(4):
            accumulate(square_grads, start_index + offset, weight_grads[offset])
        return (asking_piece, key_part)

    def expand_step(upstream_low, inputs, start_index, kept_state):
        partial_value, up_grad, down_grad = expand_back(
            upstream_low, inputs, wide_low, start_index, kept_state
        )
        accumulate(wide_grads, start_index, up_grad)
        accumulate(wide_grads, start_index + 1, down_grad)
        return partial_value

    encoder_kept = []
    encoded_pieces = []
    for micro_index in range(MICRO):
        row_start = micro_index * per_block
        source_block = source[row_start : row_start + per_block]
        allowed = key_mask(lengths[row_start : row_start + per_block, 0])
        partial_value, attend_kept = attend_forward(
            source_block, source_block, square_low, 0, allowed, head_size
        )
        hidden, hidden_kept = layer_norm(
            add_branch(own_half(source_block).astype(jnp.float32), partial_value),
            gain_rows[0],
            bias_rows[0],
        )
        hidden_low = low_rows(hidden)
        partial_value, expand_kept = expand_forward(hidden_low, wide_low, 0)
        memory, memory_kept = layer_norm(
            add_branch(hidden, partial_value), gain_rows[1], bias_rows[1]
        )
        encoded_pieces.append(low_rows(memory))
        encoder_kept.append((attend_kept, hidden_kept, hidden_low, expand_kept, memory_kept))
    memory_all = jnp.concatenate(encoded_pieces, axis=0)
    moved_memory, moved_target = (
        lax.all_to_all(by_peer(memory_all), "dp", split_axis=0, concat_axis=0, tiled=True),
        lax.all_to_all(by_peer(target), "dp", split_axis=0, concat_axis=0, tiled=True),
    )
    moved_memory = flatten(moved_memory)
    moved_target = flatten(moved_target)
    decoded_parts = []
    memory_back = []
    target_back = []
    for micro_index in range(MICRO):
        row_start = micro_index * per_block
        target_block = moved_target[row_start : row_start + per_block]
        memory_block = moved_memory[row_start : row_start + per_block]
        counts = moved_lengths[row_start : row_start + per_block]
        self_mask = key_mask(counts[:, 1]) & causal[None]
        cross_attention_mask = key_mask(counts[:, 0])
        partial_value, self_kept = attend_forward(
            target_block, target_block, square_low, 4, self_mask, head_size
        )
        first_norm, first_kept = layer_norm(
            add_branch(own_half(target_block).astype(jnp.float32), partial_value),
            gain_rows[2],
            bias_rows[2],
        )
        first_low = low_rows(first_norm)
        partial_value, cross_kept = attend_forward(
            first_low, memory_block, square_low, 8, cross_attention_mask, head_size
        )
        second_norm, second_kept = layer_norm(
            add_branch(first_norm, partial_value), gain_rows[3], bias_rows[3]
        )
        second_low = low_rows(second_norm)
        partial_value, expand_kept = expand_forward(second_low, wide_low, 2)
        output, output_kept = layer_norm(
            add_branch(second_norm, partial_value), gain_rows[4], bias_rows[4]
        )
        decoded_parts.append(identity(rounded(output)))
        upstream = norm_step(
            own_half(cotangent[row_start : row_start + per_block]).astype(jnp.float32),
            4,
            output_kept,
        )
        upstream = add_branch(upstream, expand_step(low_rows(upstream), second_low, 2, expand_kept))
        upstream = norm_step(upstream, 3, second_kept)
        asking_piece, key_part = attend_step(
            low_rows(upstream), first_low, memory_block, 8, cross_kept
        )
        asking_piece, key_part = share_total((asking_piece, key_part))
        memory_back.append(low_rows(key_part))
        upstream = norm_step(upstream + asking_piece, 2, first_kept)
        asking_piece, key_part = attend_step(
            low_rows(upstream), target_block, target_block, 4, self_kept
        )
        target_back.append(low_rows(add_branch(upstream, asking_piece + key_part)))
    returned_memory, returned_target = (
        lax.all_to_all(
            jnp.concatenate(memory_back, axis=0).reshape(
                peer_count, per_peer, slot_count, model_width
            ),
            "dp",
            split_axis=0,
            concat_axis=0,
            tiled=True,
        ),
        lax.all_to_all(
            jnp.concatenate(target_back, axis=0).reshape(
                peer_count, per_peer, slot_count, model_width
            ),
            "dp",
            split_axis=0,
            concat_axis=0,
            tiled=True,
        ),
    )
    memory_gradient = jnp.take(flatten(returned_memory), home_place, axis=0)
    target_grad = jnp.take(flatten(returned_target), home_place, axis=0).astype(jnp.float32)
    source_parts = []
    for micro_index in range(MICRO):
        row_start = micro_index * per_block
        source_block = source[row_start : row_start + per_block]
        attend_kept, hidden_kept, hidden_low, expand_kept, memory_kept = encoder_kept[micro_index]
        upstream = norm_step(
            own_half(memory_gradient[row_start : row_start + per_block]).astype(jnp.float32),
            1,
            memory_kept,
        )
        upstream = add_branch(upstream, expand_step(low_rows(upstream), hidden_low, 0, expand_kept))
        upstream = norm_step(upstream, 0, hidden_kept)
        asking_piece, key_part = attend_step(
            low_rows(upstream), source_block, source_block, 0, attend_kept
        )
        source_parts.append(identity(add_branch(upstream, asking_piece + key_part)))
    square_grad = jnp.stack(square_grads)
    wide_grad = jnp.stack(wide_grads)
    norm_grad = jnp.stack(gain_grads + bias_grads)
    square_grad, wide_grad, norm_grad = (
        lax.psum_scatter(square_grad, "dp", scatter_dimension=1, tiled=True),
        lax.psum_scatter(wide_grad, "dp", scatter_dimension=1, tiled=True),
        lax.psum_scatter(norm_grad, "dp", scatter_dimension=1, tiled=True),
    )
    row_square, row_wide, norm_grad = lax.psum(
        (
            jnp.sum(square_grad * square_grad, axis=2),
            jnp.sum(wide_grad * wide_grad, axis=2),
            norm_grad,
        ),
        "mp",
    )
    square_rows_new = 0.5 * square_rows + 0.5 * (row_square / model_width)
    wide_rows_new = 0.5 * wide_rows + 0.5 * (row_wide / FF)
    col_square, col_wide, level_square, level_wide = lax.psum(
        (
            jnp.sum(square_grad * square_grad, axis=1),
            jnp.sum(wide_grad * wide_grad, axis=1),
            jnp.sum(square_rows_new, axis=1),
            jnp.sum(wide_rows_new, axis=1),
        ),
        "dp",
    )
    square_cols_new = 0.5 * square_cols + 0.5 * (col_square / model_width)
    wide_cols_new = 0.5 * wide_cols + 0.5 * (col_wide / model_width)
    square_second = (
        square_rows_new[:, :, None]
        * square_cols_new[:, None, :]
        / (level_square / model_width)[:, None, None]
    )
    wide_second = (
        wide_rows_new[:, :, None]
        * wide_cols_new[:, None, :]
        / (level_wide / model_width)[:, None, None]
    )
    updated_square_masters = square_master - RATE * square_grad * lax.rsqrt(square_second)
    wide_new = wide_master - RATE * wide_grad * lax.rsqrt(wide_second)
    norm_second_new = 0.5 * gain_offset_moment + 0.5 * norm_grad * norm_grad
    norm_new = norm_master - NORM_RATE * norm_grad * lax.rsqrt(norm_second_new)
    return (
        jnp.concatenate(decoded_parts, axis=0),
        jnp.concatenate(source_parts, axis=0),
        target_grad,
        square_grad,
        square_rows_new,
        square_cols_new,
        updated_square_masters,
        rounded(updated_square_masters),
        wide_grad,
        wide_rows_new,
        wide_cols_new,
        wide_new,
        rounded(wide_new),
        norm_grad,
        norm_second_new,
        norm_new,
        rounded(norm_new),
    )


def solution(mesh):
    return jax.shard_map(
        shards,
        mesh=mesh,
        in_specs=(
            P("dp", None, None),
            P("dp", None, None),
            P("dp", None),
            P("dp"),
            P("dp", None, None),
            P(None, "dp", "mp"),
            P(None, "dp", "mp"),
            P(None, "dp"),
            P(None, "dp"),
            P(None, "mp"),
            P(None, "dp"),
            P(None, "mp"),
            P(None, "dp"),
        ),
        out_specs=(
            P("dp", "mp", None),
            P("dp", "mp", None),
            P("dp", None, None),
            P(None, "dp", "mp"),
            P(None, "dp"),
            P(None, "mp"),
            P(None, "dp", "mp"),
            P(None, "dp", "mp"),
            P(None, "dp", "mp"),
            P(None, "dp"),
            P(None, "mp"),
            P(None, "dp", "mp"),
            P(None, "dp", "mp"),
            P(None, "dp"),
            P(None, "dp"),
            P(None, "dp"),
            P(None, "dp"),
        ),
        check_vma=False,
    )
```

profile of v0, /device:TPU:0, one launch (start us, length us, event | category | flops | bytes accessed | tf_op | source)
XLA Modules:
  0.0 1187.9 jit_solution(5546146388518825497)
XLA Ops:
  10.0 72.2 %all-gather.4.cloned.1.call-done = bf16[12,512,256]{2,1,0:T(8,128)(2,1)} async-done(((bf16[12,32,256]{2,1,0:T(8,128)(2,1)}), bf16[12,512,256]{2,1,0:T(8,128)(2,1)}) %all-gather.4.cloned.1.call-update) | async-done | bytes 3145744 | tf_op jit(solution)/shard_map/all_gather | solution.py:205
  107.8 4.8 all-to-all-start.1
  113.3 41.5 %all-gather = bf16[16,32,10]{1,2,0:T(8,128)(2,1)S(1)} all-gather(bf16[1,32,10]{1,2,0:T(8,128)(2,1)S(1)} %convert_bitcast_fusion), channel_id=1, replica_groups=mesh['dp'=16,'mp'=2] {'dp'}, dimensions={0}, use_global_device_ids=true | all-gather | bytes 10880 | tf_op jit(solution)/shard_map/all_gather | solution.py:207
  168.2 24.7 %all-gather.6.cloned.1.call-done = bf16[4,512,1024]{2,1,0:T(8,128)(2,1)} async-done(((bf16[4,32,1024]{2,1,0:T(8,128)(2,1)}), bf16[4,512,1024]{2,1,0:T(8,128)(2,1)}) %all-gather.6.cloned.1.call-update) | async-done | bytes 4194320 | tf_op jit(solution)/shard_map/all_gather | solution.py:206
  195.8 2.3 fusion.113
  198.4 6.0 reduce-scatter.32.cloned.1.call-done
  213.4 8.6 reduce-scatter.36.cloned.1.call-done
  232.2 6.8 all-to-all-start
  241.7 5.2 all-to-all-done
  246.9 3.5 all-to-all-start.2
  295.3 2.4 fusion.395
  302.6 7.6 reduce-scatter.38.cloned.1.call-done
  316.0 2.3 fusion.401
  333.5 8.2 reduce-scatter.40.cloned.1.call-done
  360.2 3.4 reduce-scatter.48.cloned.1.call-done
  392.6 2.4 multiply_reduce_fusion.13
  403.8 2.3 fusion.114
  442.4 2.3 multiply_reduce_fusion.12
  503.6 6.8 all-to-all-start.3
  518.4 4.6 all-to-all-start.4
  556.9 2.3 multiply_reduce_fusion.15
  573.7 3.7 reduce-scatter.60.cloned.1.call-done
  628.4 2.6 stack.85
  661.3 9.6 copy.986
  678.6 3.6 pad_maximum_fusion
  683.6 26.5 %reduce-scatter.76.cloned.1.call-done = f32[32,10]{1,0:T(8,128)} async-done(((f32[512,10]{1,0:T(8,128)}), f32[32,10]{1,0:T(8,128)}) %reduce-scatter.76.cloned.1.call-update) | async-done | bytes 1296
  711.0 5.8 reduce-scatter.58.cloned.1.call-done
  716.8 11.6 reduce-scatter.62.cloned.1.call-done
  730.2 179.5 %reduce-scatter.72.cloned.1.call-done = f32[12,32,256]{2,0,1:T(8,128)} async-done(((f32[12,512,256]{2,0,1:T(8,128)}), f32[12,32,256]{2,0,1:T(8,128)}) %reduce-scatter.72.cloned.1.call-update) | async-done | bytes 393232 | tf_op jit(solution)/shard_map/reduce_scatter | solution.py:367
  912.9 179.8 %reduce-scatter.74.cloned.1.call-done = f32[4,32,1024]{2,1,0:T(8,128)} async-done(((f32[4,512,1024]{2,1,0:T(8,128)}), f32[4,32,1024]{2,1,0:T(8,128)}) %reduce-scatter.74.cloned.1.call-update) | async-done | bytes 524304 | tf_op jit(solution)/shard_map/reduce_scatter | solution.py:368
  1094.0 3.4 all-reduce.1
  1098.2 77.5 %all-reduce = (f32[12,256]{1,0:T(8,128)S(1)}, f32[12]{0:T(128)S(1)}, f32[4,1024]{1,0:T(4,128)S(1)}, f32[4]{0:T(128)S(1)}) all-reduce(f32[12,256]{1,0:T(8,128)S(1)} %get-tuple-element.109, f32[12]{0:T(128)S(1)} %get-tuple-element.167, f32[4,1024]{1,0:T(4,128)S(1)} %get-tuple-element.107, ...), channel_id=1, replica_groups=mesh['dp'=16,'mp'=2] {'dp'}, use_global_device_ids=true, to_apply=%region_86.88 | all-reduce | flops 7184 | bytes 57472 | tf_op jit(solution)/shard_map/psum | solution.py:381
  (832 shorter events, 446.8 us)
Async XLA Ops:
  7.2 75.0 %all-gather.4.cloned.1.call-start = ((), (), s32[]{:S(2)}) async-start(), calls=%async_computation.30 | async-start | bytes 3342336 | tf_op jit(solution)/shard_map/all_gather | solution.py:205
  9.0 154.3 %reduce-scatter.30.cloned.1.call-start = ((), (), s32[]{:S(2)}) async-start(), calls=%async_computation.32 | async-start | bytes 196608 | tf_op jit(solution)/shard_map/reduce_scatter | solution.py:185
  94.3 72.9 %reduce-scatter.34.cloned.1.call-start = ((), (), s32[]{:S(2)}) async-start(), calls=%async_computation.35 | async-start | bytes 196608 | tf_op jit(solution)/shard_map/reduce_scatter | solution.py:185
  102.5 90.4 %all-gather.6.cloned.1.call-start = ((), (), s32[]{:S(2)}) async-start(), calls=%async_computation.33 | async-start | bytes 4456448 | tf_op jit(solution)/shard_map/all_gather | solution.py:206
  107.8 53.0 %all-to-all-start.1 = ((s32[16,1,2]{2,1,0:T(1,128)}), s32[16,1,2]{2,1,0:T(1,128)}, u32[]{:S(2)}, u32[]{:S(2)}) async-start(s32[16,1,2]{2,1,0:T(1,128)} %copy.786), calls=%async_computation.1 | async-start | bytes 16384 | tf_op jit(solution)/shard_map/all_to_all | solution.py:202
  112.6 91.8 %reduce-scatter.32.cloned.1.call-start = ((), (), s32[]{:S(2)}) async-start(), calls=%async_computation.34 | async-start | bytes 196608 | tf_op jit(solution)/shard_map/reduce_scatter | solution.py:185
  198.1 23.9 %reduce-scatter.36.cloned.1.call-start = ((), (), s32[]{:S(2)}) async-start(), calls=%async_computation.36 | async-start | bytes 196608 | tf_op jit(solution)/shard_map/reduce_scatter | solution.py:185
  232.2 14.7 %all-to-all-start = ((bf16[16,1,8,512]{3,2,1,0:T(8,128)(2,1)}), bf16[16,1,8,512]{3,2,1,0:T(8,128)(2,1)S(1)}, u32[]{:S(2)}, u32[]{:S(2)}) async-start(bf16[16,1,8,512]{3,2,1,0:T(8,128)(2,1)} %get-tuple-element.247), calls=%async_computation | async-start | bytes 262144 | tf_op jit(solution)/shard_map/all_to_all | solution.py:273
  246.9 26.0 %all-to-all-start.2 = ((bf16[16,1,8,512]{3,2,1,0:T(8,128)(2,1)}), bf16[16,1,8,512]{3,2,1,0:T(8,128)(2,1)S(1)}, u32[]{:S(2)}, u32[]{:S(2)}) async-start(bf16[16,1,8,512]{3,2,1,0:T(8,128)(2,1)} %get-tuple-element.248), calls=%async_computation.7 | async-start | bytes 262144 | tf_op jit(solution)/shard_map/all_to_all | solution.py:272
  250.4 38.1 %reduce-scatter.28.cloned.1.call-start = ((), (), s32[]{:S(2)}) async-start(), calls=%async_computation.31 | async-start | bytes 196608 | tf_op jit(solution)/shard_map/reduce_scatter | solution.py:185
  262.8 38.6 %reduce-scatter.42.cloned.1.call-start = ((), (), s32[]{:S(2)}) async-start(), calls=%async_computation.39 | async-start | bytes 196608 | tf_op jit(solution)/shard_map/reduce_scatter | solution.py:185
  288.5 21.8 %reduce-scatter.38.cloned.1.call-start = ((), (), s32[]{:S(2)}) async-start(), calls=%async_computation.37 | async-start | bytes 196608 | tf_op jit(solution)/shard_map/reduce_scatter | solution.py:185
  301.3 30.4 %reduce-scatter.44.cloned.1.call-start = ((), (), s32[]{:S(2)}) async-start(), calls=%async_computation.40 | async-start | bytes 196608 | tf_op jit(solution)/shard_map/reduce_scatter | solution.py:185
  322.0 19.8 %reduce-scatter.40.cloned.1.call-start = ((), (), s32[]{:S(2)}) async-start(), calls=%async_computation.38 | async-start | bytes 196608 | tf_op jit(solution)/shard_map/reduce_scatter | solution.py:185
  331.4 32.2 %reduce-scatter.48.cloned.1.call-start = ((), (), s32[]{:S(2)}) async-start(), calls=%async_computation.42 | async-start | bytes 196608 | tf_op jit(solution)/shard_map/reduce_scatter | solution.py:185
  354.8 35.9 %reduce-scatter.46.cloned.1.call-start = ((), (), s32[]{:S(2)}) async-start(), calls=%async_computation.41 | async-start | bytes 196608 | tf_op jit(solution)/shard_map/reduce_scatter | solution.py:185
  360.1 32.5 %reduce-scatter.64.cloned.1.call-start = ((), (), s32[]{:S(2)}) async-start(), calls=%async_computation.50 | async-start | bytes 196608 | tf_op jit(solution)/shard_map/reduce_scatter | solution.py:185
  383.8 26.2 %reduce-scatter.50.cloned.1.call-start = ((), (), s32[]{:S(2)}) async-start(), calls=%async_computation.43 | async-start | bytes 196608 | tf_op jit(solution)/shard_map/reduce_scatter | solution.py:185
  390.6 24.7 %reduce-scatter.52.cloned.1.call-start = ((), (), s32[]{:S(2)}) async-start(), calls=%async_computation.44 | async-start | bytes 196608 | tf_op jit(solution)/shard_map/reduce_scatter | solution.py:185
  406.2 36.2 %reduce-scatter.68.cloned.1.call-start = ((), (), s32[]{:S(2)}) async-start(), calls=%async_computation.52 | async-start | bytes 196608 | tf_op jit(solution)/shard_map/reduce_scatter | solution.py:185
  432.4 66.9 %reduce-scatter.54.cloned.1.call-start = ((), (), s32[]{:S(2)}) async-start(), calls=%async_computation.45 | async-start | bytes 196608 | tf_op jit(solution)/shard_map/reduce_scatter | solution.py:185
  442.3 68.1 %reduce-scatter.66.cloned.1.call-start = ((), (), s32[]{:S(2)}) async-start(), calls=%async_computation.51 | async-start | bytes 196608 | tf_op jit(solution)/shard_map/reduce_scatter | solution.py:185
  486.1 24.4 %reduce-scatter.70.cloned.1.call-start = ((), (), s32[]{:S(2)}) async-start(), calls=%async_computation.53 | async-start | bytes 196608 | tf_op jit(solution)/shard_map/reduce_scatter | solution.py:185
  503.6 14.8 %all-to-all-start.3 = ((bf16[16,1,8,512]{3,2,1,0:T(8,128)(2,1)}), bf16[16,1,8,512]{3,2,1,0:T(8,128)(2,1)}, u32[]{:S(2)}, u32[]{:S(2)}) async-start(bf16[16,1,8,512]{3,2,1,0:T(8,128)(2,1)} %copy.886), calls=%async_computation.17 | async-start | bytes 262144 | tf_op jit(solution)/shard_map/all_to_all | solution.py:326
  518.4 15.1 %all-to-all-start.4 = ((bf16[16,1,8,512]{3,2,1,0:T(8,128)(2,1)}), bf16[16,1,8,512]{3,2,1,0:T(8,128)(2,1)S(1)}, u32[]{:S(2)}, u32[]{:S(2)}) async-start(bf16[16,1,8,512]{3,2,1,0:T(8,128)(2,1)} %copy.959), calls=%async_computation.26 | async-start | bytes 262144 | tf_op jit(solution)/shard_map/all_to_all | solution.py:335
  523.0 33.8 %reduce-scatter.56.cloned.1.call-start = ((), (), s32[]{:S(2)}) async-start(), calls=%async_computation.46 | async-start | bytes 196608 | tf_op jit(solution)/shard_map/reduce_scatter | solution.py:185
  547.9 29.5 %reduce-scatter.60.cloned.1.call-start = ((), (), s32[]{:S(2)}) async-start(), calls=%async_computation.48 | async-start | bytes 196608 | tf_op jit(solution)/shard_map/reduce_scatter | solution.py:185
  568.5 141.7 %reduce-scatter.76.cloned.1.call-start = ((), (), s32[]{:S(2)}) async-start(), calls=%async_computation.56 | async-start | bytes 278528
  632.7 84.1 %reduce-scatter.58.cloned.1.call-start = ((), (), s32[]{:S(2)}) async-start(), calls=%async_computation.47 | async-start | bytes 196608 | tf_op jit(solution)/shard_map/reduce_scatter | solution.py:185
  638.2 90.2 %reduce-scatter.62.cloned.1.call-start = ((), (), s32[]{:S(2)}) async-start(), calls=%async_computation.49 | async-start | bytes 196608 | tf_op jit(solution)/shard_map/reduce_scatter | solution.py:185
  645.3 264.4 %reduce-scatter.72.cloned.1.call-start = ((), (), s32[]{:S(2)}) async-start(), calls=%async_computation.54 | async-start | bytes 8912896 | tf_op jit(solution)/shard_map/reduce_scatter | solution.py:367
  671.0 421.7 %reduce-scatter.74.cloned.1.call-start = ((), (), s32[]{:S(2)}) async-start(), calls=%async_computation.55 | async-start | bytes 8912896 | tf_op jit(solution)/shard_map/reduce_scatter | solution.py:368
  (171 other events, 6166.8 us)
Sparse Core Ops, SparseCore 0:
  11.4 70.7 all-gather.3
  94.4 6.6 reduce-scatter.29
  103.9 8.6 reduce-scatter.33
  115.8 77.0 all-gather.5
  198.3 6.0 reduce-scatter.31
  213.3 8.6 reduce-scatter.35
  262.9 8.7 reduce-scatter.27
  288.6 8.7 reduce-scatter.41
  301.4 8.7 reduce-scatter.37
  322.1 8.6 reduce-scatter.43
  333.1 8.6 reduce-scatter.39
  354.9 8.6 reduce-scatter.47
  365.8 8.6 reduce-scatter.45
  383.9 8.6 reduce-scatter.63
  395.2 8.6 reduce-scatter.49
  406.6 8.6 reduce-scatter.51
  432.6 8.6 reduce-scatter.67
  443.9 8.6 reduce-scatter.53
  486.2 8.6 reduce-scatter.65
  497.6 8.6 reduce-scatter.69
  548.0 8.8 reduce-scatter.55
  568.6 8.6 reduce-scatter.59
  632.8 77.3 reduce-scatter.75
  712.9 3.8 reduce-scatter.57
  719.7 8.6 reduce-scatter.61
  730.6 178.9 reduce-scatter.71
  912.5 180.2 reduce-scatter.73
where the time goes:
time: 1210 us; the launch traced here: 1190 us
  waiting for transfers between devices  550 us (45%)
  matrix products  177 us (15%)
  blocking collectives  163 us (13%)
  local copies, waits for them, and re-layouts  153 us (13%)
  other arithmetic  100 us (8%)
  starting transfers between devices  28.1 us (2%)
  between operations  16.9 us (1%)
    reduce_scatter x1, waiting for transfers between devices, shards(): lax.psum_scatter(wide_grad, 'dp', scatter_dimension=1, tiled=True)  180 us
    reduce_scatter x1, waiting for transfers between devices, shards(): lax.psum_scatter(square_grad, 'dp', scatter_dimension=1, tiled=True)  179 us
    psum x1, blocking collectives, shards(): lax.psum((jnp.sum(square_grad * square_grad, axis=1), jnp.sum(wide_grad *...  77.5 us
    all_gather x1, waiting for transfers between devices, shards(): lax.all_gather(rounded(square_master), 'dp', axis=1, tiled=True)  72.2 us
    reduce_scatter x22, waiting for transfers between devices, share_total(): lax.psum_scatter(partial_value, 'mp', scatter_dimension=1, tiled=True)  59 us
    dot_general x32, matrix products, project_back(): jnp.einsum('cxk,ak->cxa', input_tensor, weight_matrix, preferred_element_...  47.4 us
    dot_general x32, matrix products, outer_sum(): jnp.einsum('zmb,zmf->bf', first_factor_array, second_factor_array, prefer...  43.6 us
    all_gather x1, blocking collectives, shards(): lax.all_gather(rounded(norm_master), 'dp', axis=1, tiled=True)  41.5 us
  transfers between devices with their start and end apart: 32, of which 18 were waited for; matrix products, arithmetic and copies ran while one was open for 23% of the time, Pallas kernels for 0%

commit v1 on v0

--- a/solution.py
+++ b/solution.py
@@ -1,6 +1,10 @@
+import types
+
 import jax
 import jax.numpy as jnp
 from jax import lax
+from jax.experimental import pallas as pl
+from jax.experimental.pallas import tpu as pltpu
 from jax.sharding import PartitionSpec as P
 
 FF = 2048
@@ -424,9 +428,1185 @@
     )
 
 
+SQUARE, WIDE = 0, 1
+LANES = 128
+TOKENS = 256
+BLOCK = 128
+CHUNK = 64
+MESH_IDS = pl.DeviceIdType.MESH
+NEG = -1000000000.0
+OUTSIDE = -3.0e38
+ENC_UNITS = ((SQUARE, 0), (WIDE, 0), (WIDE, 1))
+DEC_UNITS = ((SQUARE, 0), (SQUARE, 1), (WIDE, 0), (WIDE, 1))
+ALL_UNITS = ((0, 0), (0, 1), (0, 2), (1, 0), (1, 1), (1, 2), (1, 3))
+
+
+def mm(a, b):
+    return jnp.dot(a, b, preferred_element_type=jnp.float32)
+
+
+def mm_nt(a, b):
+    return lax.dot_general(a, b, (((1,), (1,)), ((), ())), preferred_element_type=jnp.float32)
+
+
+def mm_tn(a, b):
+    return lax.dot_general(a, b, (((0,), (0,)), ((), ())), preferred_element_type=jnp.float32)
+
+
+def repeat(count, body):
+    lax.fori_loop(0, count, lambda i, carry: (body(i), carry)[1], 0)
+
+
+def aligned(i, size):
+    return pl.ds(pl.multiple_of(i * size, size), size)
+
+
+def unit_mats(role, u):
+    kind, i = (ENC_UNITS, DEC_UNITS)[role][u]
+    if kind == SQUARE:
+        return kind, i, 4 * i + 4 * role
+    return kind, i, i + 2 * role
+
+
+def named(refs, *groups):
+    return types.SimpleNamespace(**dict(zip([name for group in groups for name in group], refs)))
+
+
+class Sems:
+    def __init__(self, send, recv, count):
+        self.send, self.recv, self.count, self.names = send, recv, count, {}
+
+    def at(self, name):
+        i = self.names.setdefault(name, len(self.names))
+        assert i < self.count
+        return self.send.at[i], self.recv.at[i]
+
+
+SEM_COUNT = 120
+(
+    S_AX,
+    S_AY,
+    S_COT,
+    S_DEC,
+    S_DM,
+    S_DT,
+    S_FX,
+    S_FY,
+    S_M,
+    S_MEMORY,
+    S_NG,
+    S_NORM,
+    S_RA,
+    S_RB,
+    S_ROWS,
+    S_RQ,
+    S_SA,
+    S_SB,
+    S_SG,
+    S_SOURCE,
+    S_ST,
+    S_T,
+    S_TARGET,
+    S_TT,
+    S_Z,
+) = range(25)
+
+SCRATCH = dict(
+    WS=((8, 4, 2, 2, 32, 256), jnp.bfloat16),
+    WW=((2, 4, 2, 2, 32, 1024), jnp.bfloat16),
+    GS=((8, 4, 2, 2, 32, 256), jnp.bfloat16),
+    GW=((2, 4, 2, 2, 32, 1024), jnp.bfloat16),
+    SB=((12, 32, 256), jnp.bfloat16),
+    WB=((4, 32, 1024), jnp.bfloat16),
+    R1AS=((8, 2, 2, 32, 256), jnp.bfloat16),
+    R1BS=((8, 2, 2, 32, 256), jnp.bfloat16),
+    R1AW=((2, 2, 2, 32, 1024), jnp.bfloat16),
+    R1BW=((2, 2, 2, 32, 1024), jnp.bfloat16),
+    R2AS=((8, 2, 32, 256), jnp.bfloat16),
+    R2BS=((8, 2, 32, 256), jnp.bfloat16),
+    R2AW=((2, 2, 32, 1024), jnp.bfloat16),
+    R2BW=((2, 2, 32, 1024), jnp.bfloat16),
+    R3S=((2, 12, 32, 256), jnp.bfloat16),
+    R3W=((2, 4, 32, 1024), jnp.bfloat16),
+    NB=((16, 16, LANES), jnp.bfloat16),
+    RL=((16, 16, LANES), jnp.float32),
+    NORM=((16, 512), jnp.float32),
+    EXT=((BLOCK, LANES), jnp.float32),
+    SEXT=((BLOCK, 640), jnp.bfloat16),
+    XEXT=((BLOCK, 640), jnp.bfloat16),
+    TSEND=((8, 16, 640), jnp.bfloat16),
+    TREC=((16, 16, 640), jnp.bfloat16),
+    COT2=((BLOCK, 512), jnp.bfloat16),
+    COT=((TOKENS, 512), jnp.float32),
+    XT=((TOKENS, 512), jnp.bfloat16),
+    MSEND=((8, 2, 16, 512), jnp.bfloat16),
+    MREC=((2, 2, 4, 16, 512), jnp.bfloat16),
+    DMSEND=((2, 2, 4, 16, 512), jnp.bfloat16),
+    MG=((8, 2, 16, 512), jnp.bfloat16),
+    DTSEND=((16, 16, 512), jnp.bfloat16),
+    TG=((8, 16, 512), jnp.bfloat16),
+    DSEND=((BLOCK, 512), jnp.bfloat16),
+    DREC=((BLOCK, 512), jnp.bfloat16),
+    SGSEND=((BLOCK, 512), jnp.float32),
+    SGREC=((BLOCK, 512), jnp.float32),
+    PERMT=((2, BLOCK, BLOCK), jnp.bfloat16),
+    ALLOW=((2, 2, BLOCK, TOKENS), jnp.float32),
+    FILL=((BLOCK, TOKENS), jnp.float32),
+    Q=((2, TOKENS, 256), jnp.bfloat16),
+    K=((2, TOKENS, 256), jnp.bfloat16),
+    V=((2, TOKENS, 256), jnp.bfloat16),
+    O=((2, TOKENS, 256), jnp.bfloat16),
+    PROB=((2, 4, BLOCK, TOKENS), jnp.float32),
+    DO=((TOKENS, 256), jnp.bfloat16),
+    DQ=((TOKENS, 256), jnp.bfloat16),
+    DK=((TOKENS, 256), jnp.bfloat16),
+    DV=((TOKENS, 256), jnp.bfloat16),
+    U=((TOKENS, 1024), jnp.float32),
+    ACT=((TOKENS, 1024), jnp.bfloat16),
+    DU=((TOKENS, 1024), jnp.bfloat16),
+    RES=((TOKENS, 512), jnp.float32),
+    LOW=((3, TOKENS, 512), jnp.bfloat16),
+    XH=((3, TOKENS, 512), jnp.float32),
+    RSD=((3, TOKENS, 1), jnp.float32),
+    GRAD=((TOKENS, 512), jnp.float32),
+    GLOW=((TOKENS, 512), jnp.bfloat16),
+    PS=((2, TOKENS, 512), jnp.float32),
+    PR=((2, TOKENS, 512), jnp.float32),
+    NGR=((4, 16, LANES), jnp.float32),
+    NG=((16, 16, LANES), jnp.float32),
+    ST=((7, 16, 8, LANES), jnp.float32),
+    RQ=((BLOCK, LANES), jnp.float32),
+    RQR=((BLOCK, LANES), jnp.float32),
+    TT=((7, 8, LANES), jnp.float32),
+    TTR=((7, 8, LANES), jnp.float32),
+)
+
+INPUTS = dict(
+    lengths=0,
+    destinations=0,
+    source=0,
+    target=0,
+    cotangent=0,
+    square=0,
+    wide=0,
+    norm=0,
+    square_rows=0,
+    wide_rows=0,
+)
+OUTPUTS = dict(
+    o_dec=((BLOCK, 512), jnp.bfloat16),
+    o_src=((BLOCK, 512), jnp.float32),
+    o_tgt=((BLOCK, 512), jnp.float32),
+    o_gs=((12, 32, 256), jnp.float32),
+    o_gw=((4, 32, 1024), jnp.float32),
+    o_cs=((12, 256), jnp.float32),
+    o_cw=((4, 1024), jnp.float32),
+    o_rq=((BLOCK, LANES), jnp.float32),
+    o_rl=((16, LANES), jnp.float32),
+    o_tt=((7, 8, LANES), jnp.float32),
+    o_ng=((16, LANES), jnp.float32),
+)
+
+
+def exchange_kernel(*refs):
+    r = named(refs, INPUTS, OUTPUTS, SCRATCH)
+    sems = Sems(refs[-2], refs[-1], SEM_COUNT)
+    d = lax.axis_index("dp")
+    c = lax.axis_index("mp")
+    z = lax.div(d, 4)
+    yx = lax.rem(d, 4)
+    y = lax.div(yx, 2)
+    x = lax.rem(yx, 2)
+    role = lax.rem(z, 2)
+    x_mate = d + 1 - 2 * x
+    y_mate = d + 2 - 4 * y
+    partner = d + 4 - 8 * role
+    bf, f32 = jnp.bfloat16, jnp.float32
+
+    G = (r.GS, r.GW)
+    R1A, R1B = (r.R1AS, r.R1AW), (r.R1BS, r.R1BW)
+    R2A, R2B = (r.R2AS, r.R2AW), (r.R2BS, r.R2BW)
+
+    def z_mate(k):
+        zz = lax.rem(z + k, 4)
+        return zz, zz * 4 + yx
+
+    def copy(src, dst, name, dev, core=None):
+        send, recv = sems.at(name)
+        return pltpu.make_async_remote_copy(
+            src_ref=src,
+            dst_ref=dst,
+            send_sem=send,
+            recv_sem=recv,
+            device_id=(dev, c if core is None else core),
+            device_id_type=MESH_IDS,
+        )
+
+    def wait_in(dst, name):
+        copy(dst, dst, name, x_mate).wait_recv()
+
+    def wait_out(src, name):
+        copy(src, src, name, x_mate).wait_send()
+
+    def unit(buf, kind, i):
+        if kind == SQUARE:
+            return buf[0], (slice(4 * i, 4 * i + 4),)
+        return buf[1], (i,)
+
+    def part(buf, kind, i, *rest):
+        ref, lead = unit(buf, kind, i)
+        return ref.at[lead + rest]
+
+    barrier = pltpu.get_barrier_semaphore()
+    for k in range(1, 16):
+        pl.semaphore_signal(
+            barrier, inc=1, device_id=(lax.rem(d + k, 16), c), device_id_type=MESH_IDS
+        )
+    pl.semaphore_signal(barrier, inc=1, device_id=(d, 1 - c), device_id_type=MESH_IDS)
+
+    for j in range(12):
+        r.SB[j] = r.square[j].astype(bf)
+    for j in range(4):
+        r.WB[j] = r.wide[j].astype(bf)
+
+    def own_weights(first_s, count, first_w):
+        for j in range(count):
+            r.WS[j, z, y, x] = r.SB[first_s + j]
+        for j in range(2):
+            r.WW[j, z, y, x] = r.WB[first_w + j]
+
+    pl.when(role == 0)(lambda: own_weights(0, 4, 0))
+    pl.when(role == 1)(lambda: own_weights(4, 8, 2))
+
+    lane = lax.broadcasted_iota(jnp.int32, (8, LANES), 1)
+    for s in range(16):
+        r.EXT[8 * s : 8 * s + 8, :] = jnp.where(
+            lane < 32,
+            r.lengths[s, 0],
+            jnp.where(lane < 64, r.lengths[s, 1], r.destinations[s]),
+        ).astype(f32)
+    ext_low = r.EXT[...].astype(bf)
+    r.SEXT[:, 0:512] = r.source[...]
+    r.SEXT[:, 512:640] = ext_low
+
+    row_id = lax.broadcasted_iota(jnp.int32, (BLOCK, BLOCK), 0)
+    col_id = lax.broadcasted_iota(jnp.int32, (BLOCK, BLOCK), 1)
+    col_z = 2 * (col_id >> 6) + 1 - ((col_id >> 3) & 1)
+    col_dev = (col_z * 4 + ((col_id >> 4) & 3)).astype(f32)
+    same_slot = (row_id & 7) == (col_id & 7)
+
+    def perm_of(dest_column):
+        return jnp.where((dest_column == col_dev) & same_slot, 1.0, 0.0)
+
+    perm_f = perm_of(r.EXT[:, 64:65])
+    r.PERMT[0] = perm_f.astype(bf)
+    perm = perm_f.T.astype(bf)
+    r.TSEND[:, :, 0:512] = mm(perm, r.target[...]).astype(bf).reshape(8, 16, 512)
+    r.TSEND[:, :, 512:640] = mm(perm, ext_low).astype(bf).reshape(8, 16, LANES)
+
+    r.NORM[...] = jnp.zeros((16, 512), f32)
+    r.NORM[0:10, 0:32] = r.norm[...]
+    shift = lax.rem(d, 4) * 32
+    r.NB[d] = pltpu.roll(r.NORM[:, 0:LANES], shift, 1).astype(bf)
+    r.RL[d] = jnp.zeros((16, LANES), f32)
+    r.RL[d, 0:12, 0:32] = r.square_rows[...]
+    r.RL[d, 12:16, 0:32] = r.wide_rows[...]
+
+    pl.semaphore_wait(barrier, 16)
+
+    def z_sends(my_role):
+        for u in range(4):
+            for k in (1, 2, 3):
+                target_role = my_role ^ (k & 1)
+                if u >= (3, 4)[target_role]:
+                    continue
+                kind, i, j = unit_mats(target_role, u)
+                src = r.SB.at[j : j + 4] if kind == SQUARE else r.WB.at[j]
+                copy(src, z_slot(kind, i), (S_Z, u, k), z_mate(k)[1]).start()
+            if u == 0:
+                early(my_role)
+
+    def z_slot(kind, i):
+        if kind == SQUARE:
+            return r.WS.at[4 * i : 4 * i + 4, z, y, x]
+        return r.WW.at[i, z, y, x]
+
+    def early(my_role):
+        for k in range(1, 16):
+            dev = lax.rem(d + k, 16)
+            copy(r.NB.at[d], r.NB.at[d], S_NORM, dev).start()
+        if my_role == 1:
+            copy(r.SEXT, r.XEXT, S_SOURCE, partner).start()
+        for t in range(8):
+            dev = (2 * (t // 4) + 1) * 4 + t % 4
+            send = copy(r.TSEND.at[t], r.TREC.at[d], S_TARGET, dev)
+            if my_role == 0:
+                send.start()
+            else:
+                pl.when(dev != d)(send.start)
+
+                @pl.when(dev == d)
+                def _():
+                    r.TREC[d] = r.TSEND[t]
+
+        if my_role == 0:
+            copy(r.cotangent, r.COT2, S_COT, partner).start()
+        for k in range(1, 16):
+            dev = lax.rem(d + k, 16)
+            copy(r.RL.at[d], r.RL.at[d], S_ROWS, dev).start()
+
+    def early_sent(my_role):
+        wait_out(r.NB.at[0:15], S_NORM)
+        wait_out(r.RL.at[0:15], S_ROWS)
+        if my_role == 1:
+            wait_out(r.SEXT, S_SOURCE)
+            wait_out(r.TSEND.at[0:7], S_TARGET)
+        else:
+            wait_out(r.cotangent, S_COT)
+            wait_out(r.TSEND, S_TARGET)
+        for u in range(4):
+            for k in (1, 2, 3):
+                target_role = my_role ^ (k & 1)
+                if u < (3, 4)[target_role]:
+                    kind, i, j = unit_mats(target_role, u)
+                    wait_out(r.SB.at[j : j + 4] if kind == SQUARE else r.WB.at[j], (S_Z, u, k))
+
+    def ag_column(units, u):
+        kind, i = units[u]
+        for k in (1, 2, 3):
+            wait_in(z_slot(kind, i), (S_Z, u, k))
+        block = z_slot_of(kind, i, y, x)
+        copy(block, block, (S_AX, u), x_mate).start()
+        copy(block, block, (S_AY, u), y_mate).start()
+
+    def z_slot_of(kind, i, yy, xx, rows=slice(None)):
+        if kind == SQUARE:
+            return r.WS.at[4 * i : 4 * i + 4, rows, yy, xx]
+        return r.WW.at[i, rows, yy, xx]
+
+    def ag_forward(units, u):
+        kind, i = units[u]
+        wait_in(z_slot_of(kind, i, y, x), (S_AY, u))
+        block = z_slot_of(kind, i, 1 - y, x, slice(0, 2))
+        copy(block, block, (S_FX, u), x_mate).start()
+        wait_in(z_slot_of(kind, i, y, x), (S_AX, u))
+        block = z_slot_of(kind, i, y, 1 - x, slice(2, 4))
+        copy(block, block, (S_FY, u), y_mate).start()
+
+    def ag_finish(units, u):
+        kind, i = units[u]
+        block = z_slot_of(kind, i, y, x, slice(0, 2))
+        wait_in(block, (S_FX, u))
+        wait_in(block, (S_FY, u))
+
+    def ag_sent(units):
+        for u, (kind, i) in enumerate(units):
+            block = z_slot_of(kind, i, y, x)
+            half = z_slot_of(kind, i, y, x, slice(0, 2))
+            wait_out(block, (S_AX, u))
+            wait_out(block, (S_AY, u))
+            wait_out(half, (S_FX, u))
+            wait_out(half, (S_FY, u))
+
+    def rs_first(units, u):
+        kind, i = units[u]
+        gref, lead = unit(G, kind, i)
+        copy(
+            gref.at[lead + (slice(0, 2), 1 - y)], part(R1A, kind, i), (S_RA, u), y_mate
+        ).start()
+        copy(
+            gref.at[lead + (slice(2, 4), slice(None), 1 - x)],
+            part(R1B, kind, i),
+            (S_RB, u),
+            x_mate,
+        ).start()
+
+    def add_into(ref, index, other):
+        ref[index] = (ref[index].astype(f32) + other[...].astype(f32)).astype(bf)
+
+    def rs_second(units, u):
+        kind, i = units[u]
+        gref, lead = unit(G, kind, i)
+        ra, rb = part(R1A, kind, i), part(R1B, kind, i)
+        wait_in(ra, (S_RA, u))
+        add_into(gref, lead + (slice(0, 2), y), ra)
+        copy(
+            gref.at[lead + (slice(0, 2), y, 1 - x)], part(R2A, kind, i), (S_SA, u), x_mate
+        ).start()
+        wait_in(rb, (S_RB, u))
+        add_into(gref, lead + (slice(2, 4), slice(None), x), rb)
+        copy(
+            gref.at[lead + (slice(2, 4), 1 - y, x)], part(R2B, kind, i), (S_SB, u), y_mate
+        ).start()
+
+    def rs_third(my_role, units, u):
+        kind, i, j = unit_mats(my_role, u)
+        gref, lead = unit(G, kind, i)
+        ra, rb = part(R2A, kind, i), part(R2B, kind, i)
+        wait_in(ra, (S_SA, u))
+        add_into(gref, lead + (slice(0, 2), y, x), ra)
+        wait_in(rb, (S_SB, u))
+        add_into(gref, lead + (slice(2, 4), y, x), rb)
+        for k in (1, 2, 3):
+            slot = 1 if k == 3 else 0
+            zz, dev = z_mate(k)
+            if kind == SQUARE:
+                dst = r.R3S.at[slot, j : j + 4]
+            else:
+                dst = r.R3W.at[slot, j]
+            copy(gref.at[lead + (zz, y, x)], dst, (S_T, my_role, u, slot, k & 1), dev).start()
+
+    def rs_sent(my_role, units):
+        for u, (kind, i) in enumerate(units):
+            gref, lead = unit(G, kind, i)
+            wait_out(part(R1A, kind, i), (S_RA, u))
+            wait_out(part(R1B, kind, i), (S_RB, u))
+            wait_out(part(R2A, kind, i), (S_SA, u))
+            wait_out(part(R2B, kind, i), (S_SB, u))
+            for k in (1, 2, 3):
+                slot = 1 if k == 3 else 0
+                wait_out(gref.at[lead + (0, y, x)], (S_T, my_role, u, slot, k & 1))
+
+    def final_sum(my_role, role_of, u):
+        kind, i, j = unit_mats(role_of, u)
+        if kind == SQUARE:
+            dst = [r.R3S.at[slot, j : j + 4] for slot in (0, 1)]
+        else:
+            dst = [r.R3W.at[slot, j] for slot in (0, 1)]
+        if my_role == role_of:
+            wait_in(dst[0], (S_T, role_of, u, 0, 0))
+            gref, lead = unit(G, kind, i)
+            total = gref[lead + (z, y, x)].astype(f32) + dst[0][...].astype(f32)
+        else:
+            wait_in(dst[0], (S_T, role_of, u, 0, 1))
+            wait_in(dst[1], (S_T, role_of, u, 1, 1))
+            total = dst[0][...].astype(f32) + dst[1][...].astype(f32)
+        if kind == SQUARE:
+            r.o_gs[j : j + 4] = total
+        else:
+            r.o_gw[j] = total
+
+    def unit_stats(g):
+        role_of, u = ALL_UNITS[g]
+        kind, i, j = unit_mats(role_of, u)
+        lanes = lax.broadcasted_iota(jnp.int32, (32, LANES), 1)
+        rows = r.RQ[0:32, :]
+        if kind == SQUARE:
+            for m in range(4):
+                grad = r.o_gs[j + m]
+                sq = grad * grad
+                cols = jnp.sum(sq, axis=0, keepdims=True)
+                for h in range(2):
+                    r.ST[g, d, 2 * m + h : 2 * m + h + 1, :] = cols[:, h * LANES : (h + 1) * LANES]
+                rows = jnp.where(lanes == j + m, jnp.sum(sq, axis=1, keepdims=True), rows)
+        else:
+            grad = r.o_gw[j]
+            sq = grad * grad
+            cols = jnp.sum(sq, axis=0, keepdims=True)
+            for h in range(8):
+                r.ST[g, d, h : h + 1, :] = cols[:, h * LANES : (h + 1) * LANES]
+            rows = jnp.where(lanes == 12 + j, jnp.sum(sq, axis=1, keepdims=True), rows)
+        r.RQ[0:32, :] = rows
+        for k in range(1, 16):
+            dev = lax.rem(d + k, 16)
+            copy(r.ST.at[g, d], r.ST.at[g, d], (S_ST, g), dev).start()
+
+    def weight(kind, i, cols=None):
+        if kind == SQUARE:
+            return r.WS[i].reshape(512, 256)
+        if cols is None:
+            return r.WW[i].reshape(512, 1024)
+        return r.WW[i, :, :, :, :, cols].reshape(512, 256)
+
+    def put_square(i, value):
+        r.GS[i] = value.astype(bf).reshape(4, 2, 2, 32, 256)
+
+    def swap(number, partial):
+        slot = number % 2
+        for half in range(2):
+            rows = slice(half * BLOCK, (half + 1) * BLOCK)
+            if number >= 2:
+                wait_out(r.PS.at[slot, rows], (S_M, number - 2, half))
+            r.PS[slot, rows] = partial(rows)
+            copy(
+                r.PS.at[slot, rows], r.PR.at[slot, rows], (S_M, number, half), d, 1 - c
+            ).start()
+
+    def swapped(number, body):
+        slot = number % 2
+        for half in range(2):
+            rows = slice(half * BLOCK, (half + 1) * BLOCK)
+            wait_in(r.PR.at[slot, rows], (S_M, number, half))
+
+            def chunk(i):
+                at = pl.ds(pl.multiple_of(half * BLOCK + i * CHUNK, CHUNK), CHUNK)
+                body(at, half * (BLOCK // CHUNK) + i, r.PS[slot, at] + r.PR[slot, at])
+
+            repeat(BLOCK // CHUNK, chunk)
+
+    def swaps_sent(count):
+        for number in (count - 2, count - 1):
+            for half in range(2):
+                wait_out(r.PS.at[0, 0:BLOCK], (S_M, number, half))
+
+    def norm_forward(residual, kept, which, at):
+        centred = residual - jnp.mean(residual, axis=-1, keepdims=True)
+        spread = lax.rsqrt(jnp.mean(centred * centred, axis=-1, keepdims=True) + 1e-05)
+        normed = centred * spread
+        r.XH[kept, at] = normed
+        r.RSD[kept, at] = spread
+        return normed * r.NORM[which : which + 1, :] + r.NORM[5 + which : 6 + which, :]
+
+    def norm_backward(upstream, kept, which, at):
+        normed = r.XH[kept, at]
+        scaled = upstream * r.NORM[which : which + 1, :]
+        both = upstream * normed
+        gain_sum = jnp.sum(both, axis=0, keepdims=True)
+        bias_sum = jnp.sum(upstream, axis=0, keepdims=True)
+        for b in range(4):
+            lanes = slice(b * LANES, (b + 1) * LANES)
+            r.NGR[b, which : which + 1, :] += gain_sum[:, lanes]
+            r.NGR[b, 5 + which : 6 + which, :] += bias_sum[:, lanes]
+        return r.RSD[kept, at] * (
+            scaled
+            - jnp.mean(scaled, axis=-1, keepdims=True)
+            - normed * jnp.mean(scaled * normed, axis=-1, keepdims=True)
+        )
+
+    head_lane = lax.broadcasted_iota(jnp.int32, (1, LANES), 1)
+    first_head = jnp.where(head_lane < 64, 1.0, 0.0)
+    second_head = 1.0 - first_head
+
+    def stacked(value):
+        wide_value = value.astype(f32)
+        return jnp.concatenate([wide_value * first_head, wide_value * second_head], axis=0).astype(bf)
+
+    def unstacked(value):
+        return value[0:BLOCK] * first_head + value[BLOCK:] * second_head
+
+    def pairs(body):
+        for blk in range(2):
+            for pr in range(2):
+                body(blk, slice(blk * BLOCK, (blk + 1) * BLOCK), slice(pr * LANES, (pr + 1) * LANES), 2 * blk + pr)
+
+    def make_masks(slot, count_of, causal):
+        row = lax.broadcasted_iota(jnp.int32, (BLOCK, TOKENS), 0)
+        col = lax.broadcasted_iota(jnp.int32, (BLOCK, TOKENS), 1) & (BLOCK - 1)
+        same = (row >> 3) == (col >> 3)
+        r.FILL[...] = jnp.where(same, NEG, OUTSIDE)
+        for blk in range(2):
+            ok = same & ((col & 7).astype(f32) < count_of(blk))
+            if causal:
+                ok = ok & ((col & 7) <= (row & 7))
+            r.ALLOW[slot, blk] = jnp.where(ok, 1.0, 0.0)
+
+    def attend(kept, mask_slot):
+        def one(blk, rows, lanes, n):
+            keys = stacked(r.K[kept, rows, lanes])
+            scores = mm_nt(r.Q[kept, rows, lanes], keys) * 0.125
+            scores = jnp.where(r.ALLOW[mask_slot, blk] > 0.5, scores, r.FILL[...])
+            halves = []
+            for h in range(2):
+                s = scores[:, h * BLOCK : (h + 1) * BLOCK]
+                e = jnp.exp(s - jnp.max(s, axis=-1, keepdims=True))
+                halves.append(e / jnp.sum(e, axis=-1, keepdims=True))
+            probs = jnp.concatenate(halves, axis=1)
+            r.PROB[kept, n] = probs
+            r.O[kept, rows, lanes] = mm(
+                probs.astype(bf), stacked(r.V[kept, rows, lanes])
+            ).astype(bf)
+
+        pairs(one)
+
+    def attend_back(kept):
+        def one(blk, rows, lanes, n):
+            queries = r.Q[kept, rows, lanes]
+            keys = stacked(r.K[kept, rows, lanes])
+            values = stacked(r.V[kept, rows, lanes])
+            out_grad = r.DO[rows, lanes]
+            probs = r.PROB[kept, n]
+            weighted = probs * mm_nt(out_grad, values)
+            halves = []
+            for h in range(2):
+                w = weighted[:, h * BLOCK : (h + 1) * BLOCK]
+                p = probs[:, h * BLOCK : (h + 1) * BLOCK]
+                halves.append(w - p * jnp.sum(w, axis=-1, keepdims=True))
+            score_grad = jnp.concatenate(halves, axis=1).astype(bf)
+            r.DQ[rows, lanes] = (mm(score_grad, keys) * 0.125).astype(bf)
+            r.DK[rows, lanes] = (unstacked(mm_tn(score_grad, queries)) * 0.125).astype(bf)
+            r.DV[rows, lanes] = unstacked(mm_tn(probs.astype(bf), out_grad)).astype(bf)
+
+        pairs(one)
+
+    def project_all(kept, base, queries, keys):
+        r.Q[kept] = mm(queries, weight(SQUARE, base)).astype(bf)
+        r.K[kept] = mm(keys, weight(SQUARE, base + 1)).astype(bf)
+        r.V[kept] = mm(keys, weight(SQUARE, base + 2)).astype(bf)
+
+    def attention_out(kept, base):
+        return lambda rows: mm_nt(r.O[kept, rows], weight(SQUARE, base + 3))
+
+    def attention_back_start(kept, base):
+        upstream = r.GLOW[...]
+        put_square(base + 3, mm_tn(upstream, r.O[kept]))
+        r.DO[...] = mm(upstream, weight(SQUARE, base + 3)).astype(bf)
+        attend_back(kept)
+
+    def attention_grads(base, queries, keys):
+        put_square(base, mm_tn(queries, r.DQ[...]))
+        put_square(base + 1, mm_tn(keys, r.DK[...]))
+        put_square(base + 2, mm_tn(keys, r.DV[...]))
+
+    def query_side(base):
+        return lambda rows: mm_nt(r.DQ[rows], weight(SQUARE, base))
+
+    def key_side(base):
+        return lambda rows: mm_nt(r.DK[rows], weight(SQUARE, base + 1)) + mm_nt(
+            r.DV[rows], weight(SQUARE, base + 2)
+        )
+
+    def all_sides(base):
+        return lambda rows: query_side(base)(rows) + key_side(base)(rows)
+
+    def expand(inputs):
+        def one(n):
+            cols = aligned(n, 256)
+            hidden = mm(inputs, weight(WIDE, 0, cols))
+            r.U[:, cols] = hidden
+            bent = jnp.tanh(0.7978845608 * (hidden + 0.044715 * hidden * hidden * hidden))
+            r.ACT[:, cols] = (0.5 * hidden * (1.0 + bent)).astype(bf)
+
+        repeat(4, one)
+
+    def contract(rows):
+        return mm_nt(r.ACT[rows], weight(WIDE, 1))
+
+    def expand_back_down():
+        upstream = r.GLOW[...]
+
+        def one(n):
+            cols = aligned(n, 256)
+            r.GW[1, :, :, :, :, cols] = (
+                mm_tn(upstream, r.ACT[:, cols]).astype(bf).reshape(4, 2, 2, 32, 256)
+            )
+
+        repeat(4, one)
+
+    def expand_back_up(inputs):
+        upstream = r.GLOW[...]
+
+        def one(n):
+            cols = aligned(n, 256)
+            active_grad = mm(upstream, weight(WIDE, 1, cols)).astype(bf).astype(f32)
+            hidden = r.U[:, cols]
+            square = hidden * hidden
+            bent = jnp.tanh(0.7978845608 * (hidden + 0.044715 * hidden * square))
+            slope = 0.5 * (1.0 + bent) + 0.5 * hidden * (1.0 - bent * bent) * 0.7978845608 * (
+                1.0 + 3.0 * 0.044715 * square
+            )
+            hidden_grad = (active_grad * slope).astype(bf)
+            r.DU[:, cols] = hidden_grad
+            r.GW[0, :, :, :, :, cols] = (
+                mm_tn(inputs, hidden_grad).astype(bf).reshape(4, 2, 2, 32, 256)
+            )
+
+        repeat(4, one)
+
+    def expand_input(rows):
+        return mm_nt(r.DU[rows], weight(WIDE, 0))
+
+    def clear_sums():
+        r.NGR[...] = jnp.zeros((4, 16, LANES), f32)
+        r.RQ[...] = jnp.zeros((BLOCK, LANES), f32)
+
+    def read_norms():
+        wait_in(r.NB.at[0:15], S_NORM)
+        for b in range(4):
+            total = r.NB[4 * b].astype(f32)
+            for i in range(1, 4):
+                total = total + r.NB[4 * b + i].astype(f32)
+            r.NORM[:, b * LANES : (b + 1) * LANES] = total
+
+    def encoder():
+        units = ENC_UNITS
+        z_sends(0)
+        clear_sums()
+        wait_in(r.XEXT, S_SOURCE)
+        r.XT[0:BLOCK] = r.source[...]
+        r.XT[BLOCK:] = r.XEXT[:, 0:512]
+        def counts(blk):
+            return r.EXT[:, 0:1] if blk == 0 else r.XEXT[:, 512:640].astype(f32)[:, 0:1]
+
+        make_masks(0, counts, False)
+        r.PERMT[1] = perm_of(r.XEXT[:, 512:640].astype(f32)[:, 64:65]).astype(bf)
+        ag_column(units, 0)
+        read_norms()
+        ag_column(units, 1)
+        ag_forward(units, 0)
+        ag_column(units, 2)
+        ag_finish(units, 0)
+        x_in = r.XT[...]
+        project_all(0, 0, x_in, x_in)
+        attend(0, 0)
+        swap(0, attention_out(0, 0))
+        ag_forward(units, 1)
+
+        def first(at, n, total):
+            hidden = norm_forward(r.XT[at].astype(f32) + total, 0, 0, at)
+            r.RES[at] = hidden
+            r.LOW[0, at] = hidden.astype(bf)
+
+        swapped(0, first)
+        ag_finish(units, 1)
+        expand(r.LOW[0])
+        ag_forward(units, 2)
+        ag_finish(units, 2)
+        swap(1, contract)
+
+        def second(at, n, total):
+            r.LOW[1, at] = norm_forward(r.RES[at] + total, 1, 1, at).astype(bf)
+
+        swapped(1, second)
+        for jj in range(2):
+            block = r.LOW[1, jj * BLOCK : (jj + 1) * BLOCK]
+            r.MSEND[:, jj] = mm_tn(r.PERMT[jj], block).astype(bf).reshape(8, 16, 512)
+        zz = lax.div(z, 2)
+        for t in range(8):
+            dev = (2 * (t // 4) + 1) * 4 + t % 4
+            copy(r.MSEND.at[t], r.MREC.at[zz, :, yx], S_MEMORY, dev).start()
+
+        wait_in(r.DREC, S_DEC)
+        r.o_dec[...] = r.DREC[...]
+        wait_in(r.MG, S_DM)
+        for jj in range(2):
+            r.GRAD[jj * BLOCK : (jj + 1) * BLOCK] = mm(
+                r.PERMT[jj], r.MG[:, jj].reshape(BLOCK, 512)
+            )
+
+        def back_one(i):
+            at = aligned(i, CHUNK)
+            value = norm_backward(r.GRAD[at], 1, 1, at)
+            r.GRAD[at] = value
+            r.GLOW[at] = value.astype(bf)
+
+        repeat(TOKENS // CHUNK, back_one)
+        expand_back_down()
+        rs_first(units, 2)
+        expand_back_up(r.LOW[0])
+        rs_first(units, 1)
+        swap(2, expand_input)
+
+        def back_two(at, n, total):
+            value = norm_backward(r.GRAD[at] + total, 0, 0, at)
+            r.GRAD[at] = value
+            r.GLOW[at] = value.astype(bf)
+
+        swapped(2, back_two)
+        attention_back_start(0, 0)
+        attention_grads(0, r.XT[...], r.XT[...])
+        rs_first(units, 0)
+        swap(3, all_sides(0))
+        rs_second(units, 2)
+
+        def back_three(at, n, total):
+            r.GRAD[at] = r.GRAD[at] + total
+
+        swapped(3, back_three)
+        r.o_src[...] = r.GRAD[0:BLOCK]
+        r.SGSEND[...] = r.GRAD[BLOCK:]
+        copy(r.SGSEND, r.SGREC, S_SG, partner).start()
+        send_norm_sums()
+        rs_second(units, 1)
+        rs_third(0, units, 2)
+        rs_second(units, 0)
+        rs_third(0, units, 1)
+        rs_third(0, units, 0)
+        wait_out(r.MSEND, S_MEMORY)
+        wait_out(r.SGSEND, S_SG)
+        swaps_sent(4)
+        take_target(0)
+        for g in (6, 5, 4, 2, 1, 3, 0):
+            final_sum(0, *ALL_UNITS[g])
+            unit_stats(g)
+        ag_sent(units)
+        rs_sent(0, units)
+        early_sent(0)
+
+    def send_norm_sums():
+        r.NG[d] = r.NGR[z]
+        for k in range(1, 16):
+            dev = lax.rem(d + k, 16)
+            copy(r.NGR.at[lax.div(dev, 4)], r.NG.at[d], S_NG, dev).start()
+
+    def take_target(my_role):
+        if my_role == 0:
+            wait_in(r.TG, S_DT)
+        else:
+            wait_in(r.TG.at[0:7], S_DT)
+        r.o_tgt[...] = mm(r.PERMT[0], r.TG[...].reshape(BLOCK, 512))
+
+    def decoder():
+        units = DEC_UNITS
+        z_sends(1)
+        clear_sums()
+        wait_in(r.TREC.at[0:15], S_TARGET)
+        wait_in(r.COT2, S_COT)
+        cot = r.COT
+
+        def place(i):
+            at = aligned(i, 32)
+            both = jnp.concatenate(
+                [
+                    r.cotangent[at].astype(f32).reshape(4, 1, 8, 512),
+                    r.COT2[at].astype(f32).reshape(4, 1, 8, 512),
+                ],
+                axis=1,
+            )
+            cot[aligned(i, CHUNK)] = both.reshape(CHUNK, 512)
+
+        repeat(4, place)
+        r.XT[...] = r.TREC[:, :, 0:512].reshape(TOKENS, 512)
+
+        def counts(which):
+            def get(blk):
+                ext = r.TREC[8 * blk : 8 * blk + 8, :, 512:640].reshape(BLOCK, LANES)
+                return ext.astype(f32)[:, 32 * which : 32 * which + 1]
+
+            return get
+
+        make_masks(0, counts(1), True)
+        make_masks(1, counts(0), False)
+        ag_column(units, 0)
+        read_norms()
+        ag_column(units, 1)
+        ag_forward(units, 0)
+        ag_column(units, 2)
+        ag_column(units, 3)
+        ag_finish(units, 0)
+        x_in = r.XT[...]
+        project_all(0, 0, x_in, x_in)
+        attend(0, 0)
+        swap(0, attention_out(0, 0))
+        ag_forward(units, 1)
+
+        def first(at, n, total):
+            hidden = norm_forward(r.XT[at].astype(f32) + total, 0, 2, at)
+            r.RES[at] = hidden
+            r.LOW[0, at] = hidden.astype(bf)
+
+        swapped(0, first)
+        ag_finish(units, 1)
+        ag_forward(units, 2)
+        r.Q[1] = mm(r.LOW[0], weight(SQUARE, 4)).astype(bf)
+        wait_in(r.MREC, S_MEMORY)
+        memory = r.MREC[...].reshape(TOKENS, 512)
+        r.K[1] = mm(memory, weight(SQUARE, 5)).astype(bf)
+        r.V[1] = mm(memory, weight(SQUARE, 6)).astype(bf)
+        attend(1, 1)
+        swap(1, attention_out(1, 4))
+        ag_forward(units, 3)
+
+        def second(at, n, total):
+            hidden = norm_forward(r.RES[at] + total, 1, 3, at)
+            r.RES[at] = hidden
+            r.LOW[1, at] = hidden.astype(bf)
+
+        swapped(1, second)
+        ag_finish(units, 2)
+        expand(r.LOW[1])
+        ag_finish(units, 3)
+        swap(2, contract)
+
+        def third(at, n, total):
+            out = norm_forward(r.RES[at] + total, 2, 4, at)
+            rows = aligned(n, 32)
+            split = out.reshape(4, 2, 8, 512)
+            r.o_dec[rows] = split[:, 0].reshape(32, 512).astype(bf)
+            r.DSEND[rows] = split[:, 1].reshape(32, 512).astype(bf)
+            value = norm_backward(cot[at], 2, 4, at)
+            r.GRAD[at] = value
+            r.GLOW[at] = value.astype(bf)
+
+        swapped(2, third)
+        expand_back_down()
+        rs_first(units, 3)
+        copy(r.DSEND, r.DREC, S_DEC, partner).start()
+        expand_back_up(r.LOW[1])
+        rs_first(units, 2)
+        swap(3, expand_input)
+
+        def back_two(at, n, total):
+            value = norm_backward(r.GRAD[at] + total, 1, 3, at)
+            r.GRAD[at] = value
+            r.GLOW[at] = value.astype(bf)
+
+        swapped(3, back_two)
+        attention_back_start(1, 4)
+        swap(4, key_side(4))
+        attention_grads(4, r.LOW[0], r.MREC[...].reshape(TOKENS, 512))
+
+        def back_memory(at, n, total):
+            r.LOW[2, at] = total.astype(bf)
+
+        swapped(4, back_memory)
+        r.DMSEND[...] = r.LOW[2].reshape(2, 2, 4, 16, 512)
+        my_t = lax.div(z, 2) * 4 + yx
+        for t in range(8):
+            dev = (2 * (t // 4)) * 4 + t % 4
+            copy(r.DMSEND.at[t // 4, :, t % 4], r.MG.at[my_t], S_DM, dev).start()
+        rs_first(units, 1)
+        swap(5, query_side(4))
+        rs_second(units, 3)
+
+        def back_three(at, n, total):
+            value = norm_backward(r.GRAD[at] + total, 0, 2, at)
+            r.GRAD[at] = value
+            r.GLOW[at] = value.astype(bf)
+
+        swapped(5, back_three)
+        attention_back_start(0, 0)
+        attention_grads(0, r.XT[...], r.XT[...])
+        rs_first(units, 0)
+        swap(6, all_sides(0))
+        rs_second(units, 2)
+
+        def back_four(at, n, total):
+            r.DTSEND[aligned(n, 4)] = (
+                (r.GRAD[at] + total).astype(bf).reshape(4, 16, 512)
+            )
+
+        swapped(6, back_four)
+        for k in range(1, 16):
+            dev = lax.rem(d + k, 16)
+            copy(r.DTSEND.at[dev], r.TG.at[my_t], S_DT, dev).start()
+        r.TG[my_t] = r.DTSEND[d]
+        send_norm_sums()
+        rs_third(1, units, 3)
+        rs_second(units, 1)
+        rs_third(1, units, 2)
+        rs_second(units, 0)
+        rs_third(1, units, 1)
+        rs_third(1, units, 0)
+        take_target(1)
+        wait_in(r.SGREC, S_SG)
+        r.o_src[...] = r.SGREC[...]
+        wait_out(r.DTSEND.at[0:15], S_DT)
+        wait_out(r.MG, S_DM)
+        wait_out(r.DSEND, S_DEC)
+        swaps_sent(7)
+        for g in (6, 5, 4, 2, 1, 3, 0):
+            final_sum(1, *ALL_UNITS[g])
+            unit_stats(g)
+        ag_sent(units)
+        rs_sent(1, units)
+        early_sent(1)
+
+    pl.when(role == 0)(encoder)
+    pl.when(role == 1)(decoder)
+
+    copy(r.RQ, r.RQR, S_RQ, d, 1 - c).start()
+    wait_in(r.NG.at[0:15], S_NG)
+    total = r.NG[0]
+    for i in range(1, 16):
+        total = total + r.NG[i]
+    r.o_ng[...] = pltpu.roll(total, lax.rem(LANES - shift, LANES), 1)
+    wait_in(r.RL.at[0:15], S_ROWS)
+    total = r.RL[0]
+    for i in range(1, 16):
+        total = total + r.RL[i]
+    r.o_rl[...] = jnp.broadcast_to(jnp.sum(total, axis=1, keepdims=True), (16, LANES))
+    for g in (6, 5, 4, 2, 1, 3, 0):
+        wait_in(r.ST.at[g, 0:15], (S_ST, g))
+        total = r.ST[g, 0]
+        for i in range(1, 16):
+            total = total + r.ST[g, i]
+        r.TT[g] = jnp.broadcast_to(jnp.sum(total, axis=1, keepdims=True), (8, LANES))
+        role_of, u = ALL_UNITS[g]
+        kind, _, j = unit_mats(role_of, u)
+        for h in range(8):
+            if kind == SQUARE:
+                r.o_cs[j + h // 2 : j + h // 2 + 1, (h % 2) * LANES : (h % 2 + 1) * LANES] = total[h : h + 1]
+            else:
+                r.o_cw[j : j + 1, h * LANES : (h + 1) * LANES] = total[h : h + 1]
+    copy(r.TT, r.TTR, S_TT, d, 1 - c).start()
+    wait_in(r.RQR, S_RQ)
+    r.o_rq[...] = r.RQ[...] + r.RQR[...]
+    wait_in(r.TTR, S_TT)
+    r.o_tt[...] = r.TT[...] + r.TTR[...]
+    wait_out(r.RQ, S_RQ)
+    wait_out(r.TT, S_TT)
+    wait_out(r.NG.at[0:15], S_NG)
+    for g in range(7):
+        wait_out(r.ST.at[g, 0:15], (S_ST, g))
+
+
+UPDATE_INPUTS = dict(
+    square=0,
+    wide=0,
+    norm=0,
+    square_rows=0,
+    square_cols=0,
+    wide_rows=0,
+    wide_cols=0,
+    moment=0,
+)
+UPDATE_OUTPUTS = dict(
+    decoded=((16, 4, 512), jnp.bfloat16),
+    source_grad=((16, 4, 512), jnp.float32),
+    target_grad=((16, 8, 512), jnp.float32),
+    square_grad=((12, 32, 256), jnp.float32),
+    square_rows_new=((12, 32), jnp.float32),
+    square_cols_new=((12, 256), jnp.float32),
+    square_new=((12, 32, 256), jnp.float32),
+    square_copy=((12, 32, 256), jnp.bfloat16),
+    wide_grad=((4, 32, 1024), jnp.float32),
+    wide_rows_new=((4, 32), jnp.float32),
+    wide_cols_new=((4, 1024), jnp.float32),
+    wide_new=((4, 32, 1024), jnp.float32),
+    wide_copy=((4, 32, 1024), jnp.bfloat16),
+    norm_grad=((10, 32), jnp.float32),
+    norm_second_new=((10, 32), jnp.float32),
+    norm_new=((10, 32), jnp.float32),
+    norm_copy=((10, 32), jnp.bfloat16),
+)
+
+
+def update_kernel(*refs):
+    r = named(refs, OUTPUTS, UPDATE_INPUTS, UPDATE_OUTPUTS, dict(rows_pad=0))
+    c = lax.axis_index("mp")
+    bf, f32 = jnp.bfloat16, jnp.float32
+
+    def own_half(value):
+        value = value.astype(f32).reshape(16, 8, 512)
+        return jnp.where(c == 0, value[:, 0:4], value[:, 4:8])
+
+    r.decoded[...] = own_half(r.o_dec[...]).astype(bf)
+    r.source_grad[...] = own_half(r.o_src[...])
+    r.target_grad[...] = r.o_tgt[...].reshape(16, 8, 512)
+    pad = r.rows_pad
+    pad[...] = jnp.zeros((BLOCK, LANES), f32)
+    pad[0:12, 0:32] = r.square_rows[...]
+    pad[12:16, 0:32] = r.wide_rows[...]
+    lanes = lax.broadcasted_iota(jnp.int32, (BLOCK, LANES), 1)
+    widths = jnp.where(lanes < 12, 1.0 / 512, 1.0 / FF)
+    rows_new = 0.5 * pad[...].T + 0.5 * (r.o_rq[...] * widths)
+    rows_back = rows_new.T
+    r.square_rows_new[...] = rows_back[0:12, 0:32]
+    r.wide_rows_new[...] = rows_back[12:16, 0:32]
+    square_cols = 0.5 * r.square_cols[...] + 0.5 * (r.o_cs[...] / 512)
+    wide_cols = 0.5 * r.wide_cols[...] + 0.5 * (r.o_cw[...] / 512)
+    r.square_cols_new[...] = square_cols
+    r.wide_cols_new[...] = wide_cols
+
+    def level(m, total, width):
+        return (0.5 * r.o_rl[m : m + 1, 0:1] + 0.5 * (total / width)) / 512
+
+    def update(master, grad, row, col, lvl):
+        return master - RATE * grad * lax.rsqrt(row * col / lvl)
+
+    for g, (role, u) in enumerate(ALL_UNITS):
+        kind, _, j = unit_mats(role, u)
+        if kind == SQUARE:
+            for m in range(4):
+                sums = r.o_tt[g]
+                total = sums[2 * m : 2 * m + 1, 0:1] + sums[2 * m + 1 : 2 * m + 2, 0:1]
+                grad = r.o_gs[j + m]
+                new = update(
+                    r.square[j + m],
+                    grad,
+                    rows_new[0:32, j + m : j + m + 1],
+                    square_cols[j + m : j + m + 1],
+                    level(j + m, total, 512),
+                )
+                r.square_grad[j + m] = grad
+                r.square_new[j + m] = new
+                r.square_copy[j + m] = new.astype(bf)
+        else:
+            total = jnp.sum(r.o_tt[g], axis=0, keepdims=True)[:, 0:1]
+            grad = r.o_gw[j]
+            new = update(
+                r.wide[j],
+                grad,
+                rows_new[0:32, 12 + j : 13 + j],
+                wide_cols[j : j + 1],
+                level(12 + j, total, FF),
+            )
+            r.wide_grad[j] = grad
+            r.wide_new[j] = new
+            r.wide_copy[j] = new.astype(bf)
+    norm_grad = r.o_ng[0:10, 0:32]
+    second = 0.5 * r.moment[...] + 0.5 * norm_grad * norm_grad
+    norm_new = r.norm[...] - NORM_RATE * norm_grad * lax.rsqrt(second)
+    r.norm_grad[...] = norm_grad
+    r.norm_second_new[...] = second
+    r.norm_new[...] = norm_new
+    r.norm_copy[...] = norm_new.astype(bf)
+
+
+def small_shards(
+    source,
+    target,
+    lengths,
+    destinations,
+    cotangent,
+    square_master,
+    wide_master,
+    norm_master,
+    square_rows,
+    square_cols,
+    wide_rows,
+    wide_cols,
+    gain_offset_moment,
+):
+    vmem = pl.BlockSpec(memory_space=pltpu.VMEM)
+    smem = pl.BlockSpec(memory_space=pltpu.SMEM)
+    moved = pl.pallas_call(
+        exchange_kernel,
+        out_shape=[jax.ShapeDtypeStruct(*v) for v in OUTPUTS.values()],
+        in_specs=[smem, smem] + [vmem] * 8,
+        out_specs=[vmem] * len(OUTPUTS),
+        scratch_shapes=[pltpu.VMEM(*v) for v in SCRATCH.values()]
+        + [pltpu.SemaphoreType.DMA((SEM_COUNT,)), pltpu.SemaphoreType.DMA((SEM_COUNT,))],
+        compiler_params=pltpu.CompilerParams(
+            collective_id=0, has_side_effects=True, vmem_limit_bytes=56 << 20
+        ),
+    )(
+        lengths,
+        destinations,
+        source.reshape(BLOCK, 512),
+        target.reshape(BLOCK, 512),
+        cotangent.reshape(BLOCK, 512),
+        square_master,
+        wide_master,
+        norm_master,
+        square_rows,
+        wide_rows,
+    )
+    return tuple(
+        pl.pallas_call(
+            update_kernel,
+            out_shape=[jax.ShapeDtypeStruct(*v) for v in UPDATE_OUTPUTS.values()],
+            in_specs=[vmem] * (len(OUTPUTS) + len(UPDATE_INPUTS)),
+            out_specs=[vmem] * len(UPDATE_OUTPUTS),
+            scratch_shapes=[pltpu.VMEM((BLOCK, LANES), jnp.float32)],
+            compiler_params=pltpu.CompilerParams(vmem_limit_bytes=32 << 20),
+        )(
+            *moved,
+            square_master,
+            wide_master,
+            norm_master,
+            square_rows,
+            square_cols,
+            wide_rows,
+            wide_cols,
+            gain_offset_moment,
+        )
+    )
+
+
 def solution(mesh):
     return jax.shard_map(
-        shards,
+        small_shards if dict(mesh.shape) == {"dp": 16, "mp": 2} else shards,
         mesh=mesh,
         in_specs=(
             P("dp", None, None),

time: 1210 us -> 158 us (0.13); the launches traced: 1190 us -> 157 us
  waiting for transfers between devices: 550 us -> 0 us
  matrix products: 177 us -> 0 us
  blocking collectives: 163 us -> 0 us
  Pallas kernels: 0 us -> 145 us
  local copies, waits for them, and re-layouts: 153 us -> 11.3 us
  other arithmetic: 100 us -> 0 us
  starting transfers between devices: 28.1 us -> 0 us
  between operations: 16.9 us -> 0.94 us
    reduce_scatter x24 -> x0, waiting for transfers between devices: 418 us -> none  [the longest x1 180 us: shards(): lax.psum_scatter(wide_grad, 'dp', scatter_dimension=1, tiled=True)]
    dot_general x128 -> x0, matrix products: 169 us -> none  [the longest x32 47.4 us: project_back(): jnp.einsum('cxk,ak->cxa', input_tensor, weight_matrix, preferred_element_...]
    pallas_call x0 -> x2, Pallas kernels: none -> 145 us  [the longest x1 143 us: small_shards(): pl.pallas_call(exchange_kernel, out_shape=[jax.ShapeDtypeStruct(*v) for v...]
    all_gather x2 -> x0, waiting for transfers between devices: 96.9 us -> none  [the longest x1 72.2 us: shards(): lax.all_gather(rounded(square_master), 'dp', axis=1, tiled=True)]
    all_gather x23 -> x0, blocking collectives: 82.6 us -> none  [the longest x1 41.5 us: shards(): lax.all_gather(rounded(norm_master), 'dp', axis=1, tiled=True)]
    psum x2 -> x0, blocking collectives: 80.9 us -> none  [the longest x1 77.5 us: shards(): lax.psum((jnp.sum(square_grad * square_grad, axis=1), jnp.sum(wide_grad *...]
    reshape x46 -> x0, local copies, waits for them, and re-layouts: 56.7 us -> none  [the longest x20 28.7 us: merge_heads(): input_tensor.reshape(input_tensor.shape[0], input_tensor.shape[1], input_...]
    convert_element_type x48 -> x0, local copies, waits for them, and re-layouts: 34.8 us -> none  [rounded(): return input_tensor.astype(jnp.bfloat16)]
  transfers between devices with their start and end apart: 32 -> 0, of which waited for: 18 -> 0; matrix products, arithmetic and copies ran while one was open for 23% -> 0% of each run, Pallas kernels for 0% -> 0%
where the time goes in v1:
time: 158 us; the launch traced here: 157 us
  Pallas kernels  145 us (92%)
  local copies, waits for them, and re-layouts  11.3 us (7%)
    pallas_call x1, Pallas kernels, small_shards(): pl.pallas_call(exchange_kernel, out_shape=[jax.ShapeDtypeStruct(*v) for v...  143 us
    unnamed x41, local copies, waits for them, and re-layouts  11.3 us

profile of v1, /device:TPU:0, one launch (start us, length us, event | category | flops | bytes accessed | tf_op | source)
XLA Modules:
  0.0 157.4 jit_solution(18291465026293804355)
XLA Ops:
  0.7 0.0 copy-start.19
  0.7 0.7 copy-done.19
  1.3 0.7 copy.30.refs_0_
  2.0 0.0 copy-start
  2.0 0.0 copy-start.1
  2.0 0.0 copy-start.11
  2.0 0.0 copy-start.12
  2.0 0.0 copy-start.15
  2.0 143.4 %shard_map.260 = (bf16[128,512]{1,0:T(8,128)(2,1)}, f32[128,512]{1,0:T(8,128)}, f32[128,512]{1,0:T(8,128)}, f32[12,32,256]{2,1,0:T(8,128)}, f32[4,32,1024]{2,1,0...) custom-call(s32[16,2]{1,0:T(8,128)} %copy.30.refs_0_, ...), custom_call_target="tpu_custom_call" | custom-call | tf_op jit(solution)/shard_map/pallas_call | solution.py:1563
  145.4 0.0 copy-start.18
  145.4 0.0 copy-start.9
  145.4 0.0 copy-start.8
  145.5 0.0 copy-done
  145.5 0.0 copy-done.1
  145.5 0.0 copy-done.11
  145.5 0.0 copy-done.12
  145.5 0.0 copy-done.15
  145.5 0.6 copy-done.18
  146.1 0.0 copy-done.9
  146.1 0.0 copy-done.8
  146.2 1.0 copy-done.2
  147.2 1.0 copy-done.3
  148.2 0.9 copy-done.4
  149.1 0.9 copy-done.5
  150.1 0.9 copy-done.6
  151.0 0.8 copy-done.7
  151.8 0.7 copy-done.10
  152.6 0.7 copy-done.13
  153.3 0.7 copy-done.14
  154.0 0.7 copy-done.16
  154.7 0.7 copy-done.17
  155.4 1.8 %shard_map.261 = (bf16[16,4,512]{2,1,0:T(4,128)(2,1)}, f32[16,4,512]{2,1,0:T(4,128)}, f32[16,8,512]{2,1,0:T(8,128)}, f32[12,32,256]{2,1,0:T(8,128)}, f32[12,32]{...) custom-call(bf16[128,512]{1,0:T(8,128)(2,1)S(1)} %copy-done.6, ...), custom_call_target="tpu_custom_call" | custom-call | tf_op jit(solution)/shard_map/pallas_call | solution.py:1586
  (11 shorter events, 0.0 us)
Async XLA Ops:
  0.7 0.7 copy-start.19
  2.0 143.4 %copy-start = (f32[4,32,1024]{2,1,0:T(8,128)S(1)}, f32[4,32,1024]{2,1,0:T(8,128)}, u32[]{:S(2)}) copy-start(f32[4,32,1024]{2,1,0:T(8,128)} %refs_12_.1) | copy-start | bytes 1572868
  2.0 143.5 %copy-start.1 = (f32[12,32,256]{2,1,0:T(8,128)S(1)}, f32[12,32,256]{2,1,0:T(8,128)}, u32[]{:S(2)}) copy-start(f32[12,32,256]{2,1,0:T(8,128)} %refs_11_.1) | copy-start | bytes 1179652
  2.0 143.5 %copy-start.11 = (f32[12,256]{1,0:T(8,128)S(1)}, f32[12,256]{1,0:T(8,128)}, u32[]{:S(2)}) copy-start(f32[12,256]{1,0:T(8,128)} %refs_15_.1) | copy-start | bytes 36868
  2.0 143.5 %copy-start.12 = (f32[4,1024]{1,0:T(4,128)S(1)}, f32[4,1024]{1,0:T(4,128)}, u32[]{:S(2)}) copy-start(f32[4,1024]{1,0:T(4,128)} %refs_17_.1) | copy-start | bytes 49156
  2.0 143.5 %copy-start.15 = (f32[10,32]{1,0:T(8,128)S(1)}, f32[10,32]{1,0:T(8,128)}, u32[]{:S(2)}) copy-start(f32[10,32]{1,0:T(8,128)} %refs_18_.1) | copy-start | bytes 3844
  145.4 0.7 copy-start.18
  145.4 0.7 copy-start.9
  145.4 0.7 copy-start.8
  146.2 1.0 copy-start.2
  147.2 1.0 copy-start.3
  148.2 0.9 copy-start.4
  149.1 0.9 copy-start.5
  150.1 0.9 copy-start.6
  151.0 0.8 copy-start.7
  151.8 0.7 copy-start.10
  152.6 0.7 copy-start.13
  153.3 0.7 copy-start.14
  154.0 0.7 copy-start.16
  154.7 0.7 copy-start.17

commit v2 on v1

--- a/solution.py
+++ b/solution.py
@@ -482,7 +482,8 @@
         return self.send.at[i], self.recv.at[i]
 
 
-SEM_COUNT = 120
+SEM_COUNT = 176
+NEAR_COUNT = 16
 (
     S_AX,
     S_AY,
@@ -498,18 +499,24 @@
     S_NORM,
     S_RA,
     S_RB,
-    S_ROWS,
     S_RQ,
     S_SA,
     S_SB,
     S_SG,
     S_SOURCE,
     S_ST,
+    S_SU,
+    S_NH,
+    S_EXT,
+    S_SOURCE2,
+    S_MEMORY2,
+    S_DM2,
+    S_DT2,
     S_T,
     S_TARGET,
     S_TT,
     S_Z,
-) = range(25)
+) = range(31)
 
 SCRATCH = dict(
     WS=((8, 4, 2, 2, 32, 256), jnp.bfloat16),
@@ -529,26 +536,28 @@
     R3S=((2, 12, 32, 256), jnp.bfloat16),
     R3W=((2, 4, 32, 1024), jnp.bfloat16),
     NB=((16, 16, LANES), jnp.bfloat16),
-    RL=((16, 16, LANES), jnp.float32),
+    RL=((16, LANES), jnp.float32),
     NORM=((16, 512), jnp.float32),
     EXT=((BLOCK, LANES), jnp.float32),
-    SEXT=((BLOCK, 640), jnp.bfloat16),
-    XEXT=((BLOCK, 640), jnp.bfloat16),
+    SEXT=((BLOCK, LANES), jnp.bfloat16),
+    XHALF=((2, BLOCK, 256), jnp.bfloat16),
+    XEXT=((BLOCK, LANES), jnp.bfloat16),
     TSEND=((8, 16, 640), jnp.bfloat16),
     TREC=((16, 16, 640), jnp.bfloat16),
     COT2=((BLOCK, 512), jnp.bfloat16),
     COT=((TOKENS, 512), jnp.float32),
     XT=((TOKENS, 512), jnp.bfloat16),
     MSEND=((8, 2, 16, 512), jnp.bfloat16),
-    MREC=((2, 2, 4, 16, 512), jnp.bfloat16),
+    MREC=((2, 2, 2, 4, 16, 256), jnp.bfloat16),
+    MEM=((TOKENS, 512), jnp.bfloat16),
     DMSEND=((2, 2, 4, 16, 512), jnp.bfloat16),
-    MG=((8, 2, 16, 512), jnp.bfloat16),
+    MG=((2, 8, 2, 16, 256), jnp.bfloat16),
     DTSEND=((16, 16, 512), jnp.bfloat16),
-    TG=((8, 16, 512), jnp.bfloat16),
+    TG=((2, 8, 16, 256), jnp.bfloat16),
     DSEND=((BLOCK, 512), jnp.bfloat16),
     DREC=((BLOCK, 512), jnp.bfloat16),
-    SGSEND=((BLOCK, 512), jnp.float32),
-    SGREC=((BLOCK, 512), jnp.float32),
+    SGSEND=((16, 4, 512), jnp.float32),
+    SGREC=((16, 4, 512), jnp.float32),
     PERMT=((2, BLOCK, BLOCK), jnp.bfloat16),
     ALLOW=((2, 2, BLOCK, TOKENS), jnp.float32),
     FILL=((BLOCK, TOKENS), jnp.float32),
@@ -573,11 +582,23 @@
     PS=((2, TOKENS, 512), jnp.float32),
     PR=((2, TOKENS, 512), jnp.float32),
     NGR=((4, 16, LANES), jnp.float32),
-    NG=((16, 16, LANES), jnp.float32),
-    ST=((7, 16, 8, LANES), jnp.float32),
+    NG=((4, 16, LANES), jnp.float32),
+    NH=((4, 16, LANES), jnp.float32),
+    ST=((7, 4, 8, LANES), jnp.float32),
+    SU=((7, 4, 8, LANES), jnp.float32),
     RQ=((BLOCK, LANES), jnp.float32),
     RQR=((BLOCK, LANES), jnp.float32),
     TT=((7, 8, LANES), jnp.float32),
+    SM=((12, 32, 256), jnp.float32),
+    WM=((4, 32, 1024), jnp.float32),
+    SRC=((BLOCK, 512), jnp.bfloat16),
+    TGT=((BLOCK, 512), jnp.bfloat16),
+    COT1=((BLOCK, 512), jnp.bfloat16),
+    F_DEC=((BLOCK, 512), jnp.bfloat16),
+    F_SRC=((16, 4, 512), jnp.float32),
+    F_TGT=((BLOCK, 512), jnp.float32),
+    F_GS=((12, 32, 256), jnp.float32),
+    F_GW=((4, 32, 1024), jnp.float32),
     TTR=((7, 8, LANES), jnp.float32),
 )
 
@@ -595,7 +616,7 @@
 )
 OUTPUTS = dict(
     o_dec=((BLOCK, 512), jnp.bfloat16),
-    o_src=((BLOCK, 512), jnp.float32),
+    o_src=((16, 4, 512), jnp.float32),
     o_tgt=((BLOCK, 512), jnp.float32),
     o_gs=((12, 32, 256), jnp.float32),
     o_gw=((4, 32, 1024), jnp.float32),
@@ -610,7 +631,8 @@
 
 def exchange_kernel(*refs):
     r = named(refs, INPUTS, OUTPUTS, SCRATCH)
-    sems = Sems(refs[-2], refs[-1], SEM_COUNT)
+    sems = Sems(refs[-3], refs[-2], SEM_COUNT)
+    near = refs[-1]
     d = lax.axis_index("dp")
     c = lax.axis_index("mp")
     z = lax.div(d, 4)
@@ -642,6 +664,25 @@
             device_id_type=MESH_IDS,
         )
 
+    def local(src, dst, i):
+        return pltpu.make_async_copy(src, dst, near.at[i])
+
+    my_half = pl.ds(pl.multiple_of(c * 256, 256), 256)
+
+    def hand_over(ref, name):
+        copy(ref.at[c], ref.at[c], name, d, 1 - c).start()
+        wait_in(ref.at[0], name)
+        wait_out(ref.at[0], name)
+
+    def plane_mates():
+        return (x_mate, y_mate, z * 4 + 3 - yx)
+
+    def in_order(ref, lead=()):
+        total = ref[lead + (0,)]
+        for i in range(1, 4):
+            total = total + ref[lead + (i,)]
+        return total
+
     def wait_in(dst, name):
         copy(dst, dst, name, x_mate).wait_recv()
 
@@ -657,6 +698,15 @@
         ref, lead = unit(buf, kind, i)
         return ref.at[lead + rest]
 
+    loads = [
+        local(r.target, r.TGT, 0),
+        local(r.source, r.SRC, 1),
+        local(r.square, r.SM, 2),
+        local(r.wide, r.WM, 3),
+        local(r.cotangent, r.COT1, 4),
+    ]
+    for load in loads:
+        load.start()
     barrier = pltpu.get_barrier_semaphore()
     for k in range(1, 16):
         pl.semaphore_signal(
@@ -664,10 +714,47 @@
         )
     pl.semaphore_signal(barrier, inc=1, device_id=(d, 1 - c), device_id_type=MESH_IDS)
 
+    lane = lax.broadcasted_iota(jnp.int32, (8, LANES), 1)
+    for s in range(16):
+        r.EXT[8 * s : 8 * s + 8, :] = jnp.where(
+            lane < 32,
+            r.lengths[0, s],
+            jnp.where(lane < 64, r.lengths[1, s], r.destinations[s]),
+        ).astype(f32)
+    ext_low = r.EXT[...].astype(bf)
+    r.SEXT[...] = ext_low
+
+    row_id = lax.broadcasted_iota(jnp.int32, (BLOCK, BLOCK), 0)
+    col_id = lax.broadcasted_iota(jnp.int32, (BLOCK, BLOCK), 1)
+    col_z = 2 * (col_id >> 6) + 1 - ((col_id >> 3) & 1)
+    col_dev = (col_z * 4 + ((col_id >> 4) & 3)).astype(f32)
+    same_slot = (row_id & 7) == (col_id & 7)
+
+    def perm_of(dest_column):
+        return jnp.where((dest_column == col_dev) & same_slot, 1.0, 0.0)
+
+    perm_f = perm_of(r.EXT[:, 64:65])
+    r.PERMT[0] = perm_f.astype(bf)
+    perm = perm_f.T.astype(bf)
+    loads[0].wait()
+    r.TSEND[:, :, 0:512] = mm(perm, r.TGT[...]).astype(bf).reshape(8, 16, 512)
+    r.TSEND[:, :, 512:640] = mm(perm, ext_low).astype(bf).reshape(8, 16, LANES)
+
+    r.NORM[...] = jnp.zeros((16, 512), f32)
+    r.NORM[0:10, 0:32] = r.norm[...]
+    shift = lax.rem(d, 4) * 32
+    r.NB[d] = pltpu.roll(r.NORM[:, 0:LANES], shift, 1).astype(bf)
+    r.RL[...] = jnp.zeros((16, LANES), f32)
+    r.RL[0:12, 0:32] = r.square_rows[...]
+    r.RL[12:16, 0:32] = r.wide_rows[...]
+
+    loads[1].wait()
+    loads[2].wait()
+    loads[3].wait()
     for j in range(12):
-        r.SB[j] = r.square[j].astype(bf)
+        r.SB[j] = r.SM[j].astype(bf)
     for j in range(4):
-        r.WB[j] = r.wide[j].astype(bf)
+        r.WB[j] = r.WM[j].astype(bf)
 
     def own_weights(first_s, count, first_w):
         for j in range(count):
@@ -678,65 +765,35 @@
     pl.when(role == 0)(lambda: own_weights(0, 4, 0))
     pl.when(role == 1)(lambda: own_weights(4, 8, 2))
 
-    lane = lax.broadcasted_iota(jnp.int32, (8, LANES), 1)
-    for s in range(16):
-        r.EXT[8 * s : 8 * s + 8, :] = jnp.where(
-            lane < 32,
-            r.lengths[s, 0],
-            jnp.where(lane < 64, r.lengths[s, 1], r.destinations[s]),
-        ).astype(f32)
-    ext_low = r.EXT[...].astype(bf)
-    r.SEXT[:, 0:512] = r.source[...]
-    r.SEXT[:, 512:640] = ext_low
-
-    row_id = lax.broadcasted_iota(jnp.int32, (BLOCK, BLOCK), 0)
-    col_id = lax.broadcasted_iota(jnp.int32, (BLOCK, BLOCK), 1)
-    col_z = 2 * (col_id >> 6) + 1 - ((col_id >> 3) & 1)
-    col_dev = (col_z * 4 + ((col_id >> 4) & 3)).astype(f32)
-    same_slot = (row_id & 7) == (col_id & 7)
-
-    def perm_of(dest_column):
-        return jnp.where((dest_column == col_dev) & same_slot, 1.0, 0.0)
-
-    perm_f = perm_of(r.EXT[:, 64:65])
-    r.PERMT[0] = perm_f.astype(bf)
-    perm = perm_f.T.astype(bf)
-    r.TSEND[:, :, 0:512] = mm(perm, r.target[...]).astype(bf).reshape(8, 16, 512)
-    r.TSEND[:, :, 512:640] = mm(perm, ext_low).astype(bf).reshape(8, 16, LANES)
-
-    r.NORM[...] = jnp.zeros((16, 512), f32)
-    r.NORM[0:10, 0:32] = r.norm[...]
-    shift = lax.rem(d, 4) * 32
-    r.NB[d] = pltpu.roll(r.NORM[:, 0:LANES], shift, 1).astype(bf)
-    r.RL[d] = jnp.zeros((16, LANES), f32)
-    r.RL[d, 0:12, 0:32] = r.square_rows[...]
-    r.RL[d, 12:16, 0:32] = r.wide_rows[...]
-
+    loads[4].wait()
     pl.semaphore_wait(barrier, 16)
 
-    def z_sends(my_role):
-        for u in range(4):
-            for k in (1, 2, 3):
-                target_role = my_role ^ (k & 1)
-                if u >= (3, 4)[target_role]:
-                    continue
-                kind, i, j = unit_mats(target_role, u)
-                src = r.SB.at[j : j + 4] if kind == SQUARE else r.WB.at[j]
-                copy(src, z_slot(kind, i), (S_Z, u, k), z_mate(k)[1]).start()
-            if u == 0:
-                early(my_role)
-
-    def z_slot(kind, i):
+    def z_slot(kind, i, k=0, yy=None, xx=None):
+        zz = lax.rem(z + 4 - k, 4)
+        at = (zz, y if yy is None else yy, x if xx is None else xx)
         if kind == SQUARE:
-            return r.WS.at[4 * i : 4 * i + 4, z, y, x]
-        return r.WW.at[i, z, y, x]
-
-    def early(my_role):
+            return r.WS.at[(slice(4 * i, 4 * i + 4),) + at]
+        return r.WW.at[(i,) + at]
+
+    def z_send(my_role, target_role, u):
+        kind, i, j = unit_mats(target_role, u)
+        src = r.SB.at[j : j + 4] if kind == SQUARE else r.WB.at[j]
+        for k in (2,) if my_role == target_role else (1, 3):
+            copy(src, z_slot(kind, i), (S_Z, u, k), z_mate(k)[1]).start()
+
+    def z_sent(my_role):
+        for target_role, u in ALL_UNITS:
+            kind, i, j = unit_mats(target_role, u)
+            src = r.SB.at[j : j + 4] if kind == SQUARE else r.WB.at[j]
+            for k in (2,) if my_role == target_role else (1, 3):
+                wait_out(src, (S_Z, u, k))
+
+    def send_norms():
         for k in range(1, 16):
             dev = lax.rem(d + k, 16)
             copy(r.NB.at[d], r.NB.at[d], S_NORM, dev).start()
-        if my_role == 1:
-            copy(r.SEXT, r.XEXT, S_SOURCE, partner).start()
+
+    def send_target(my_role):
         for t in range(8):
             dev = (2 * (t // 4) + 1) * 4 + t % 4
             send = copy(r.TSEND.at[t], r.TREC.at[d], S_TARGET, dev)
@@ -749,64 +806,47 @@
                 def _():
                     r.TREC[d] = r.TSEND[t]
 
-        if my_role == 0:
-            copy(r.cotangent, r.COT2, S_COT, partner).start()
-        for k in range(1, 16):
-            dev = lax.rem(d + k, 16)
-            copy(r.RL.at[d], r.RL.at[d], S_ROWS, dev).start()
-
-    def early_sent(my_role):
-        wait_out(r.NB.at[0:15], S_NORM)
-        wait_out(r.RL.at[0:15], S_ROWS)
-        if my_role == 1:
-            wait_out(r.SEXT, S_SOURCE)
-            wait_out(r.TSEND.at[0:7], S_TARGET)
-        else:
-            wait_out(r.cotangent, S_COT)
-            wait_out(r.TSEND, S_TARGET)
-        for u in range(4):
-            for k in (1, 2, 3):
-                target_role = my_role ^ (k & 1)
-                if u < (3, 4)[target_role]:
-                    kind, i, j = unit_mats(target_role, u)
-                    wait_out(r.SB.at[j : j + 4] if kind == SQUARE else r.WB.at[j], (S_Z, u, k))
+    def ag_own(units):
+        for u, (kind, i) in enumerate(units):
+            ag_plane(kind, i, u, 0)
+
+    def ag_plane(kind, i, u, k):
+        block = z_slot(kind, i, k)
+        copy(block, block, (S_AX, u, k), x_mate).start()
+        copy(block, block, (S_AY, u, k), y_mate).start()
 
     def ag_column(units, u):
         kind, i = units[u]
-        for k in (1, 2, 3):
+        for k in (1, 3, 2):
             wait_in(z_slot(kind, i), (S_Z, u, k))
-        block = z_slot_of(kind, i, y, x)
-        copy(block, block, (S_AX, u), x_mate).start()
-        copy(block, block, (S_AY, u), y_mate).start()
-
-    def z_slot_of(kind, i, yy, xx, rows=slice(None)):
-        if kind == SQUARE:
-            return r.WS.at[4 * i : 4 * i + 4, rows, yy, xx]
-        return r.WW.at[i, rows, yy, xx]
+            ag_plane(kind, i, u, k)
 
     def ag_forward(units, u):
         kind, i = units[u]
-        wait_in(z_slot_of(kind, i, y, x), (S_AY, u))
-        block = z_slot_of(kind, i, 1 - y, x, slice(0, 2))
-        copy(block, block, (S_FX, u), x_mate).start()
-        wait_in(z_slot_of(kind, i, y, x), (S_AX, u))
-        block = z_slot_of(kind, i, y, 1 - x, slice(2, 4))
-        copy(block, block, (S_FY, u), y_mate).start()
+        for k in (0, 1, 3, 2):
+            if k < 2:
+                wait_in(z_slot(kind, i), (S_AY, u, k))
+                block = z_slot(kind, i, k, yy=1 - y)
+                copy(block, block, (S_FX, u, k), x_mate).start()
+            else:
+                wait_in(z_slot(kind, i), (S_AX, u, k))
+                block = z_slot(kind, i, k, xx=1 - x)
+                copy(block, block, (S_FY, u, k), y_mate).start()
 
     def ag_finish(units, u):
         kind, i = units[u]
-        block = z_slot_of(kind, i, y, x, slice(0, 2))
-        wait_in(block, (S_FX, u))
-        wait_in(block, (S_FY, u))
+        block = z_slot(kind, i)
+        for k in (0, 1, 3, 2):
+            wait_in(block, (S_AX if k < 2 else S_AY, u, k))
+            wait_in(block, (S_FX if k < 2 else S_FY, u, k))
 
     def ag_sent(units):
         for u, (kind, i) in enumerate(units):
-            block = z_slot_of(kind, i, y, x)
-            half = z_slot_of(kind, i, y, x, slice(0, 2))
-            wait_out(block, (S_AX, u))
-            wait_out(block, (S_AY, u))
-            wait_out(half, (S_FX, u))
-            wait_out(half, (S_FY, u))
+            block = z_slot(kind, i)
+            for k in range(4):
+                wait_out(block, (S_AX, u, k))
+                wait_out(block, (S_AY, u, k))
+                wait_out(block, (S_FX if k < 2 else S_FY, u, k))
 
     def rs_first(units, u):
         kind, i = units[u]
@@ -882,9 +922,9 @@
             wait_in(dst[1], (S_T, role_of, u, 1, 1))
             total = dst[0][...].astype(f32) + dst[1][...].astype(f32)
         if kind == SQUARE:
-            r.o_gs[j : j + 4] = total
+            r.F_GS[j : j + 4] = total
         else:
-            r.o_gw[j] = total
+            r.F_GW[j] = total
 
     def unit_stats(g):
         role_of, u = ALL_UNITS[g]
@@ -893,23 +933,39 @@
         rows = r.RQ[0:32, :]
         if kind == SQUARE:
             for m in range(4):
-                grad = r.o_gs[j + m]
+                grad = r.F_GS[j + m]
                 sq = grad * grad
                 cols = jnp.sum(sq, axis=0, keepdims=True)
                 for h in range(2):
-                    r.ST[g, d, 2 * m + h : 2 * m + h + 1, :] = cols[:, h * LANES : (h + 1) * LANES]
+                    r.ST[g, z, 2 * m + h : 2 * m + h + 1, :] = cols[:, h * LANES : (h + 1) * LANES]
                 rows = jnp.where(lanes == j + m, jnp.sum(sq, axis=1, keepdims=True), rows)
         else:
-            grad = r.o_gw[j]
+            grad = r.F_GW[j]
             sq = grad * grad
             cols = jnp.sum(sq, axis=0, keepdims=True)
             for h in range(8):
-                r.ST[g, d, h : h + 1, :] = cols[:, h * LANES : (h + 1) * LANES]
+                r.ST[g, z, h : h + 1, :] = cols[:, h * LANES : (h + 1) * LANES]
             rows = jnp.where(lanes == 12 + j, jnp.sum(sq, axis=1, keepdims=True), rows)
         r.RQ[0:32, :] = rows
-        for k in range(1, 16):
-            dev = lax.rem(d + k, 16)
-            copy(r.ST.at[g, d], r.ST.at[g, d], (S_ST, g), dev).start()
+        for k in (1, 2, 3):
+            copy(r.ST.at[g, z], r.ST.at[g, z], (S_ST, g), z_mate(k)[1]).start()
+
+    def spread_unit(g):
+        wait_in(r.ST.at[g, 0:3], (S_ST, g))
+        r.SU[g, yx] = in_order(r.ST, (g,))
+        for dev in plane_mates():
+            copy(r.SU.at[g, yx], r.SU.at[g, yx], (S_SU, g), dev).start()
+
+    def store_unit(g):
+        kind, i, j = unit_mats(*ALL_UNITS[g])
+        if kind == SQUARE:
+            return local(r.F_GS.at[j : j + 4], r.o_gs.at[j : j + 4], 8 + g)
+        return local(r.F_GW.at[j], r.o_gw.at[j], 8 + g)
+
+    def finish_unit(my_role, g):
+        final_sum(my_role, *ALL_UNITS[g])
+        store_unit(g).start()
+        unit_stats(g)
 
     def weight(kind, i, cols=None):
         if kind == SQUARE:
@@ -1117,6 +1173,12 @@
 
     def clear_sums():
         r.NGR[...] = jnp.zeros((4, 16, LANES), f32)
+        sums = jnp.sum(r.RL[...], axis=1, keepdims=True)
+        rows = lax.broadcasted_iota(jnp.int32, (16, LANES), 0)
+        lanes = lax.broadcasted_iota(jnp.int32, (16, LANES), 1)
+        line = jnp.sum(jnp.where(rows == lanes, sums, 0.0), axis=0, keepdims=True)
+        for b in range(4):
+            r.NGR[b, 10:11, :] = line
         r.RQ[...] = jnp.zeros((BLOCK, LANES), f32)
 
     def read_norms():
@@ -1129,20 +1191,32 @@
 
     def encoder():
         units = ENC_UNITS
-        z_sends(0)
+        for u in range(3):
+            z_send(0, 0, u)
+        ag_own(units)
+        send_norms()
+        z_send(0, 1, 0)
+        z_send(0, 1, 1)
+        send_target(0)
+        z_send(0, 1, 2)
+        z_send(0, 1, 3)
+        copy(r.COT1, r.COT2, S_COT, partner).start()
         clear_sums()
-        wait_in(r.XEXT, S_SOURCE)
-        r.XT[0:BLOCK] = r.source[...]
-        r.XT[BLOCK:] = r.XEXT[:, 0:512]
+        ag_column(units, 0)
+        ag_forward(units, 0)
+        ag_column(units, 1)
+        wait_in(r.XEXT, S_EXT)
+        wait_in(r.XHALF.at[0], S_SOURCE)
+        hand_over(r.XHALF, S_SOURCE2)
+        r.XT[0:BLOCK] = r.SRC[...]
+        for half in range(2):
+            r.XT[BLOCK:, half * 256 : half * 256 + 256] = r.XHALF[half]
         def counts(blk):
-            return r.EXT[:, 0:1] if blk == 0 else r.XEXT[:, 512:640].astype(f32)[:, 0:1]
+            return r.EXT[:, 0:1] if blk == 0 else r.XEXT[...].astype(f32)[:, 0:1]
 
         make_masks(0, counts, False)
-        r.PERMT[1] = perm_of(r.XEXT[:, 512:640].astype(f32)[:, 64:65]).astype(bf)
-        ag_column(units, 0)
+        r.PERMT[1] = perm_of(r.XEXT[...].astype(f32)[:, 64:65]).astype(bf)
         read_norms()
-        ag_column(units, 1)
-        ag_forward(units, 0)
         ag_column(units, 2)
         ag_finish(units, 0)
         x_in = r.XT[...]
@@ -1173,15 +1247,20 @@
         zz = lax.div(z, 2)
         for t in range(8):
             dev = (2 * (t // 4) + 1) * 4 + t % 4
-            copy(r.MSEND.at[t], r.MREC.at[zz, :, yx], S_MEMORY, dev).start()
+            copy(
+                r.MSEND.at[t, :, :, my_half], r.MREC.at[c, zz, :, yx], S_MEMORY, dev
+            ).start()
 
         wait_in(r.DREC, S_DEC)
-        r.o_dec[...] = r.DREC[...]
-        wait_in(r.MG, S_DM)
+        r.F_DEC[...] = r.DREC[...]
+        local(r.F_DEC, r.o_dec, 5).start()
+        wait_in(r.MG.at[0], S_DM)
+        hand_over(r.MG, S_DM2)
         for jj in range(2):
-            r.GRAD[jj * BLOCK : (jj + 1) * BLOCK] = mm(
-                r.PERMT[jj], r.MG[:, jj].reshape(BLOCK, 512)
-            )
+            for half in range(2):
+                r.GRAD[jj * BLOCK : (jj + 1) * BLOCK, half * 256 : half * 256 + 256] = mm(
+                    r.PERMT[jj], r.MG[half, :, jj].reshape(BLOCK, 256)
+                )
 
         def back_one(i):
             at = aligned(i, CHUNK)
@@ -1212,59 +1291,99 @@
             r.GRAD[at] = r.GRAD[at] + total
 
         swapped(3, back_three)
-        r.o_src[...] = r.GRAD[0:BLOCK]
-        r.SGSEND[...] = r.GRAD[BLOCK:]
+        for target_ref, value in ((r.F_SRC, r.GRAD[0:BLOCK]), (r.SGSEND, r.GRAD[BLOCK:])):
+            value = value.reshape(16, 8, 512)
+            target_ref[...] = jnp.where(c == 0, value[:, 0:4], value[:, 4:8])
+        local(r.F_SRC, r.o_src, 6).start()
         copy(r.SGSEND, r.SGREC, S_SG, partner).start()
         send_norm_sums()
+        finish_unit(0, 6)
+        take_target(0)
         rs_second(units, 1)
         rs_third(0, units, 2)
+        finish_unit(0, 5)
         rs_second(units, 0)
+        finish_unit(0, 4)
         rs_third(0, units, 1)
+        finish_unit(0, 2)
+        finish_unit(0, 3)
         rs_third(0, units, 0)
-        wait_out(r.MSEND, S_MEMORY)
+        wait_out(r.MREC.at[0], S_MEMORY)
         wait_out(r.SGSEND, S_SG)
         swaps_sent(4)
-        take_target(0)
-        for g in (6, 5, 4, 2, 1, 3, 0):
-            final_sum(0, *ALL_UNITS[g])
-            unit_stats(g)
+        spread_norm_sums()
+        for g in (6, 5, 4):
+            spread_unit(g)
+        finish_unit(0, 1)
+        spread_unit(2)
+        spread_unit(3)
+        finish_unit(0, 0)
+        spread_unit(1)
+        spread_unit(0)
         ag_sent(units)
         rs_sent(0, units)
-        early_sent(0)
+        z_sent(0)
+        wait_out(r.NB.at[0:15], S_NORM)
+        wait_out(r.COT1, S_COT)
+        wait_out(r.TSEND, S_TARGET)
 
     def send_norm_sums():
-        r.NG[d] = r.NGR[z]
-        for k in range(1, 16):
-            dev = lax.rem(d + k, 16)
-            copy(r.NGR.at[lax.div(dev, 4)], r.NG.at[d], S_NG, dev).start()
+        r.NG[z] = r.NGR[z]
+        for k in (1, 2, 3):
+            zz, dev = z_mate(k)
+            copy(r.NGR.at[zz], r.NG.at[z], S_NG, dev).start()
+
+    def spread_norm_sums():
+        wait_in(r.NG.at[0:3], S_NG)
+        r.NH[yx] = in_order(r.NG)
+        for dev in plane_mates():
+            copy(r.NH.at[yx], r.NH.at[yx], S_NH, dev).start()
 
     def take_target(my_role):
         if my_role == 0:
-            wait_in(r.TG, S_DT)
+            wait_in(r.TG.at[0], S_DT)
         else:
-            wait_in(r.TG.at[0:7], S_DT)
-        r.o_tgt[...] = mm(r.PERMT[0], r.TG[...].reshape(BLOCK, 512))
+            wait_in(r.TG.at[0, 0:7], S_DT)
+        hand_over(r.TG, S_DT2)
+        for half in range(2):
+            r.F_TGT[:, half * 256 : half * 256 + 256] = mm(
+                r.PERMT[0], r.TG[half].reshape(BLOCK, 256)
+            )
+        local(r.F_TGT, r.o_tgt, 7).start()
 
     def decoder():
         units = DEC_UNITS
-        z_sends(1)
+        z_send(1, 0, 0)
+        copy(r.SRC.at[:, my_half], r.XHALF.at[c], S_SOURCE, partner).start()
+        copy(r.SEXT, r.XEXT, S_EXT, partner).start()
+        z_send(1, 0, 1)
+        z_send(1, 0, 2)
+        ag_own(units)
+        send_norms()
+        for u in range(2):
+            z_send(1, 1, u)
+        send_target(1)
+        for u in range(2, 4):
+            z_send(1, 1, u)
         clear_sums()
+        ag_column(units, 0)
+        ag_forward(units, 0)
+        ag_column(units, 1)
+        ag_forward(units, 1)
         wait_in(r.TREC.at[0:15], S_TARGET)
-        wait_in(r.COT2, S_COT)
         cot = r.COT
 
         def place(i):
             at = aligned(i, 32)
             both = jnp.concatenate(
                 [
-                    r.cotangent[at].astype(f32).reshape(4, 1, 8, 512),
+                    r.COT1[at].astype(f32).reshape(4, 1, 8, 512),
                     r.COT2[at].astype(f32).reshape(4, 1, 8, 512),
                 ],
                 axis=1,
             )
             cot[aligned(i, CHUNK)] = both.reshape(CHUNK, 512)
 
-        repeat(4, place)
         r.XT[...] = r.TREC[:, :, 0:512].reshape(TOKENS, 512)
 
         def counts(which):
@@ -1276,10 +1395,7 @@
 
         make_masks(0, counts(1), True)
         make_masks(1, counts(0), False)
-        ag_column(units, 0)
         read_norms()
-        ag_column(units, 1)
-        ag_forward(units, 0)
         ag_column(units, 2)
         ag_column(units, 3)
         ag_finish(units, 0)
@@ -1287,7 +1403,7 @@
         project_all(0, 0, x_in, x_in)
         attend(0, 0)
         swap(0, attention_out(0, 0))
-        ag_forward(units, 1)
+        ag_forward(units, 2)
 
         def first(at, n, total):
             hidden = norm_forward(r.XT[at].astype(f32) + total, 0, 2, at)
@@ -1295,16 +1411,20 @@
             r.LOW[0, at] = hidden.astype(bf)
 
         swapped(0, first)
+        ag_forward(units, 3)
         ag_finish(units, 1)
-        ag_forward(units, 2)
+        wait_in(r.COT2, S_COT)
+        repeat(4, place)
         r.Q[1] = mm(r.LOW[0], weight(SQUARE, 4)).astype(bf)
-        wait_in(r.MREC, S_MEMORY)
-        memory = r.MREC[...].reshape(TOKENS, 512)
+        wait_in(r.MREC.at[0], S_MEMORY)
+        hand_over(r.MREC, S_MEMORY2)
+        for half in range(2):
+            r.MEM[:, half * 256 : half * 256 + 256] = r.MREC[half].reshape(TOKENS, 256)
+        memory = r.MEM[...]
         r.K[1] = mm(memory, weight(SQUARE, 5)).astype(bf)
         r.V[1] = mm(memory, weight(SQUARE, 6)).astype(bf)
         attend(1, 1)
         swap(1, attention_out(1, 4))
-        ag_forward(units, 3)
 
         def second(at, n, total):
             hidden = norm_forward(r.RES[at] + total, 1, 3, at)
@@ -1321,7 +1441,7 @@
             out = norm_forward(r.RES[at] + total, 2, 4, at)
             rows = aligned(n, 32)
             split = out.reshape(4, 2, 8, 512)
-            r.o_dec[rows] = split[:, 0].reshape(32, 512).astype(bf)
+            r.F_DEC[rows] = split[:, 0].reshape(32, 512).astype(bf)
             r.DSEND[rows] = split[:, 1].reshape(32, 512).astype(bf)
             value = norm_backward(cot[at], 2, 4, at)
             r.GRAD[at] = value
@@ -1331,6 +1451,7 @@
         expand_back_down()
         rs_first(units, 3)
         copy(r.DSEND, r.DREC, S_DEC, partner).start()
+        local(r.F_DEC, r.o_dec, 5).start()
         expand_back_up(r.LOW[1])
         rs_first(units, 2)
         swap(3, expand_input)
@@ -1343,7 +1464,7 @@
         swapped(3, back_two)
         attention_back_start(1, 4)
         swap(4, key_side(4))
-        attention_grads(4, r.LOW[0], r.MREC[...].reshape(TOKENS, 512))
+        attention_grads(4, r.LOW[0], r.MEM[...])
 
         def back_memory(at, n, total):
             r.LOW[2, at] = total.astype(bf)
@@ -1353,7 +1474,9 @@
         my_t = lax.div(z, 2) * 4 + yx
         for t in range(8):
             dev = (2 * (t // 4)) * 4 + t % 4
-            copy(r.DMSEND.at[t // 4, :, t % 4], r.MG.at[my_t], S_DM, dev).start()
+            copy(
+                r.DMSEND.at[t // 4, :, t % 4, :, my_half], r.MG.at[c, my_t], S_DM, dev
+            ).start()
         rs_first(units, 1)
         swap(5, query_side(4))
         rs_second(units, 3)
@@ -1378,48 +1501,56 @@
         swapped(6, back_four)
         for k in range(1, 16):
             dev = lax.rem(d + k, 16)
-            copy(r.DTSEND.at[dev], r.TG.at[my_t], S_DT, dev).start()
-        r.TG[my_t] = r.DTSEND[d]
+            copy(r.DTSEND.at[dev, :, my_half], r.TG.at[c, my_t], S_DT, dev).start()
+        r.TG[c, my_t] = r.DTSEND[d, :, my_half]
         send_norm_sums()
         rs_third(1, units, 3)
         rs_second(units, 1)
         rs_third(1, units, 2)
+        finish_unit(1, 6)
         rs_second(units, 0)
         rs_third(1, units, 1)
+        finish_unit(1, 5)
+        take_target(1)
         rs_third(1, units, 0)
-        take_target(1)
+        finish_unit(1, 4)
+        finish_unit(1, 2)
         wait_in(r.SGREC, S_SG)
-        r.o_src[...] = r.SGREC[...]
-        wait_out(r.DTSEND.at[0:15], S_DT)
-        wait_out(r.MG, S_DM)
+        r.F_SRC[...] = r.SGREC[...]
+        local(r.F_SRC, r.o_src, 6).start()
+        wait_out(r.DTSEND.at[0:15, :, 0:256], S_DT)
+        wait_out(r.MG.at[0], S_DM)
         wait_out(r.DSEND, S_DEC)
         swaps_sent(7)
-        for g in (6, 5, 4, 2, 1, 3, 0):
-            final_sum(1, *ALL_UNITS[g])
-            unit_stats(g)
+        spread_norm_sums()
+        for g in (6, 5, 4):
+            spread_unit(g)
+        finish_unit(1, 3)
+        finish_unit(1, 1)
+        spread_unit(2)
+        spread_unit(3)
+        finish_unit(1, 0)
+        spread_unit(1)
+        spread_unit(0)
         ag_sent(units)
         rs_sent(1, units)
-        early_sent(1)
+        z_sent(1)
+        wait_out(r.NB.at[0:15], S_NORM)
+        wait_out(r.SEXT, S_EXT)
+        wait_out(r.XHALF.at[0], S_SOURCE)
+        wait_out(r.TSEND.at[0:7], S_TARGET)
 
     pl.when(role == 0)(encoder)
     pl.when(role == 1)(decoder)
 
     copy(r.RQ, r.RQR, S_RQ, d, 1 - c).start()
-    wait_in(r.NG.at[0:15], S_NG)
-    total = r.NG[0]
-    for i in range(1, 16):
-        total = total + r.NG[i]
+    wait_in(r.NH.at[0:3], S_NH)
+    total = in_order(r.NH)
     r.o_ng[...] = pltpu.roll(total, lax.rem(LANES - shift, LANES), 1)
-    wait_in(r.RL.at[0:15], S_ROWS)
-    total = r.RL[0]
-    for i in range(1, 16):
-        total = total + r.RL[i]
-    r.o_rl[...] = jnp.broadcast_to(jnp.sum(total, axis=1, keepdims=True), (16, LANES))
-    for g in (6, 5, 4, 2, 1, 3, 0):
-        wait_in(r.ST.at[g, 0:15], (S_ST, g))
-        total = r.ST[g, 0]
-        for i in range(1, 16):
-            total = total + r.ST[g, i]
+    r.o_rl[...] = total
+    for g in (6, 5, 4, 2, 3, 1, 0):
+        wait_in(r.SU.at[g, 0:3], (S_SU, g))
+        total = in_order(r.SU, (g,))
         r.TT[g] = jnp.broadcast_to(jnp.sum(total, axis=1, keepdims=True), (8, LANES))
         role_of, u = ALL_UNITS[g]
         kind, _, j = unit_mats(role_of, u)
@@ -1435,9 +1566,16 @@
     r.o_tt[...] = r.TT[...] + r.TTR[...]
     wait_out(r.RQ, S_RQ)
     wait_out(r.TT, S_TT)
-    wait_out(r.NG.at[0:15], S_NG)
+    wait_out(r.NG.at[0:3], S_NG)
+    wait_out(r.NH.at[0:3], S_NH)
     for g in range(7):
-        wait_out(r.ST.at[g, 0:15], (S_ST, g))
+        wait_out(r.ST.at[g, 0:3], (S_ST, g))
+        wait_out(r.SU.at[g, 0:3], (S_SU, g))
+    local(r.F_DEC, r.o_dec, 5).wait()
+    local(r.F_SRC, r.o_src, 6).wait()
+    local(r.F_TGT, r.o_tgt, 7).wait()
+    for g in range(7):
+        store_unit(g).wait()
 
 
 UPDATE_INPUTS = dict(
@@ -1481,7 +1619,7 @@
         return jnp.where(c == 0, value[:, 0:4], value[:, 4:8])
 
     r.decoded[...] = own_half(r.o_dec[...]).astype(bf)
-    r.source_grad[...] = own_half(r.o_src[...])
+    r.source_grad[...] = r.o_src[...]
     r.target_grad[...] = r.o_tgt[...].reshape(16, 8, 512)
     pad = r.rows_pad
     pad[...] = jnp.zeros((BLOCK, LANES), f32)
@@ -1499,7 +1637,7 @@
     r.wide_cols_new[...] = wide_cols
 
     def level(m, total, width):
-        return (0.5 * r.o_rl[m : m + 1, 0:1] + 0.5 * (total / width)) / 512
+        return (0.5 * r.o_rl[10:11, m : m + 1] + 0.5 * (total / width)) / 512
 
     def update(master, grad, row, col, lvl):
         return master - RATE * grad * lax.rsqrt(row * col / lvl)
@@ -1560,18 +1698,19 @@
 ):
     vmem = pl.BlockSpec(memory_space=pltpu.VMEM)
     smem = pl.BlockSpec(memory_space=pltpu.SMEM)
+    anywhere = pl.BlockSpec(memory_space=pl.ANY)
     moved = pl.pallas_call(
         exchange_kernel,
         out_shape=[jax.ShapeDtypeStruct(*v) for v in OUTPUTS.values()],
-        in_specs=[smem, smem] + [vmem] * 8,
-        out_specs=[vmem] * len(OUTPUTS),
+        in_specs=[smem, smem] + [anywhere] * 5 + [vmem] * 3,
+        out_specs=[anywhere] * 5 + [vmem] * (len(OUTPUTS) - 5),
         scratch_shapes=[pltpu.VMEM(*v) for v in SCRATCH.values()]
-        + [pltpu.SemaphoreType.DMA((SEM_COUNT,)), pltpu.SemaphoreType.DMA((SEM_COUNT,))],
+        + [pltpu.SemaphoreType.DMA((n,)) for n in (SEM_COUNT, SEM_COUNT, NEAR_COUNT)],
         compiler_params=pltpu.CompilerParams(
             collective_id=0, has_side_effects=True, vmem_limit_bytes=56 << 20
         ),
     )(
-        lengths,
+        lengths.T,
         destinations,
         source.reshape(BLOCK, 512),
         target.reshape(BLOCK, 512),
@@ -1589,7 +1728,7 @@
             in_specs=[vmem] * (len(OUTPUTS) + len(UPDATE_INPUTS)),
             out_specs=[vmem] * len(UPDATE_OUTPUTS),
             scratch_shapes=[pltpu.VMEM((BLOCK, LANES), jnp.float32)],
-            compiler_params=pltpu.CompilerParams(vmem_limit_bytes=32 << 20),
+            compiler_params=pltpu.CompilerParams(vmem_limit_bytes=60 << 20),
         )(
             *moved,
             square_master,

time: 158 us -> 134 us (0.85)
  Pallas kernels: 145 us -> 133 us
  local copies, waits for them, and re-layouts: 11.3 us -> 0 us
    pallas_call x1, Pallas kernels: 143 us -> 129 us  [small_shards(): pl.pallas_call(exchange_kernel, out_shape=[jax.ShapeDtypeStruct(*v) for v...]
    unnamed x41 -> x0, local copies, waits for them, and re-layouts: 11.3 us -> none
    pallas_call x1, Pallas kernels: 1.85 us -> 3.78 us  [small_shards(): pl.pallas_call(update_kernel, out_shape=[jax.ShapeDtypeStruct(*v) for v i...]
where the time goes in v2:
time: 134 us
  Pallas kernels  133 us (99%)
    pallas_call x1, Pallas kernels, small_shards(): pl.pallas_call(exchange_kernel, out_shape=[jax.ShapeDtypeStruct(*v) for v...  129 us
    pallas_call x1, Pallas kernels, small_shards(): pl.pallas_call(update_kernel, out_shape=[jax.ShapeDtypeStruct(*v) for v i...  3.78 us

profile of v2, /device:TPU:0, one launch (start us, length us, event | category | flops | bytes accessed | tf_op | source)
XLA Modules:
  0.0 133.9 jit_solution(18237714972624306581)
XLA Ops:
  0.7 129.2 %shard_map.260 = (bf16[128,512]{1,0:T(8,128)(2,1)}, f32[16,4,512]{2,1,0:T(4,128)}, f32[128,512]{1,0:T(8,128)}, f32[12,32,256]{2,1,0:T(8,128)}, f32[4,32,1024]{2,...) custom-call(s32[2,16]{1,0:T(2,128)} %bitcast.7, ...), custom_call_target="tpu_custom_call" | custom-call | tf_op jit(solution)/shard_map/pallas_call | solution.py:1702
  129.9 3.8 %shard_map.261 = (bf16[16,4,512]{2,1,0:T(4,128)(2,1)}, f32[16,4,512]{2,1,0:T(4,128)}, f32[16,8,512]{2,1,0:T(8,128)}, f32[12,32,256]{2,1,0:T(8,128)}, f32[12,32]{...) custom-call(bf16[128,512]{1,0:T(8,128)(2,1)} %get-tuple-element.28.r, ...), custom_call_target="tpu_custom_call" | custom-call | tf_op jit(solution)/shard_map/pallas_call | solution.py:1725

commit v3 on v2

--- a/solution.py
+++ b/solution.py
@@ -454,7 +454,7 @@
 
 
 def repeat(count, body):
-    lax.fori_loop(0, count, lambda i, carry: (body(i), carry)[1], 0)
+    lax.fori_loop(0, count, lambda i, carry: (body(i), carry)[1], 0, unroll=True)
 
 
 def aligned(i, size):
@@ -482,7 +482,7 @@
         return self.send.at[i], self.recv.at[i]
 
 
-SEM_COUNT = 176
+SEM_COUNT = 240
 NEAR_COUNT = 16
 (
     S_AX,
@@ -506,6 +506,7 @@
     S_SOURCE,
     S_ST,
     S_SU,
+    S_SV,
     S_NH,
     S_EXT,
     S_SOURCE2,
@@ -516,7 +517,7 @@
     S_TARGET,
     S_TT,
     S_Z,
-) = range(31)
+) = range(32)
 
 SCRATCH = dict(
     WS=((8, 4, 2, 2, 32, 256), jnp.bfloat16),
@@ -579,13 +580,14 @@
     RSD=((3, TOKENS, 1), jnp.float32),
     GRAD=((TOKENS, 512), jnp.float32),
     GLOW=((TOKENS, 512), jnp.bfloat16),
-    PS=((2, TOKENS, 512), jnp.float32),
-    PR=((2, TOKENS, 512), jnp.float32),
+    PS=((2, TOKENS, 512), jnp.bfloat16),
+    PR=((2, TOKENS, 512), jnp.bfloat16),
     NGR=((4, 16, LANES), jnp.float32),
     NG=((4, 16, LANES), jnp.float32),
     NH=((4, 16, LANES), jnp.float32),
     ST=((7, 4, 8, LANES), jnp.float32),
     SU=((7, 4, 8, LANES), jnp.float32),
+    SV=((16, 8, LANES), jnp.float32),
     RQ=((BLOCK, LANES), jnp.float32),
     RQR=((BLOCK, LANES), jnp.float32),
     TT=((7, 8, LANES), jnp.float32),
@@ -689,15 +691,6 @@
     def wait_out(src, name):
         copy(src, src, name, x_mate).wait_send()
 
-    def unit(buf, kind, i):
-        if kind == SQUARE:
-            return buf[0], (slice(4 * i, 4 * i + 4),)
-        return buf[1], (i,)
-
-    def part(buf, kind, i, *rest):
-        ref, lead = unit(buf, kind, i)
-        return ref.at[lead + rest]
-
     loads = [
         local(r.target, r.TGT, 0),
         local(r.source, r.SRC, 1),
@@ -705,24 +698,14 @@
         local(r.wide, r.WM, 3),
         local(r.cotangent, r.COT1, 4),
     ]
-    for load in loads:
-        load.start()
+    for i in (2, 3, 1, 0, 4):
+        loads[i].start()
     barrier = pltpu.get_barrier_semaphore()
     for k in range(1, 16):
         pl.semaphore_signal(
             barrier, inc=1, device_id=(lax.rem(d + k, 16), c), device_id_type=MESH_IDS
         )
     pl.semaphore_signal(barrier, inc=1, device_id=(d, 1 - c), device_id_type=MESH_IDS)
-
-    lane = lax.broadcasted_iota(jnp.int32, (8, LANES), 1)
-    for s in range(16):
-        r.EXT[8 * s : 8 * s + 8, :] = jnp.where(
-            lane < 32,
-            r.lengths[0, s],
-            jnp.where(lane < 64, r.lengths[1, s], r.destinations[s]),
-        ).astype(f32)
-    ext_low = r.EXT[...].astype(bf)
-    r.SEXT[...] = ext_low
 
     row_id = lax.broadcasted_iota(jnp.int32, (BLOCK, BLOCK), 0)
     col_id = lax.broadcasted_iota(jnp.int32, (BLOCK, BLOCK), 1)
@@ -733,40 +716,23 @@
     def perm_of(dest_column):
         return jnp.where((dest_column == col_dev) & same_slot, 1.0, 0.0)
 
-    perm_f = perm_of(r.EXT[:, 64:65])
-    r.PERMT[0] = perm_f.astype(bf)
-    perm = perm_f.T.astype(bf)
-    loads[0].wait()
-    r.TSEND[:, :, 0:512] = mm(perm, r.TGT[...]).astype(bf).reshape(8, 16, 512)
-    r.TSEND[:, :, 512:640] = mm(perm, ext_low).astype(bf).reshape(8, 16, LANES)
-
-    r.NORM[...] = jnp.zeros((16, 512), f32)
-    r.NORM[0:10, 0:32] = r.norm[...]
-    shift = lax.rem(d, 4) * 32
-    r.NB[d] = pltpu.roll(r.NORM[:, 0:LANES], shift, 1).astype(bf)
-    r.RL[...] = jnp.zeros((16, LANES), f32)
-    r.RL[0:12, 0:32] = r.square_rows[...]
-    r.RL[12:16, 0:32] = r.wide_rows[...]
-
-    loads[1].wait()
-    loads[2].wait()
-    loads[3].wait()
-    for j in range(12):
-        r.SB[j] = r.SM[j].astype(bf)
-    for j in range(4):
-        r.WB[j] = r.WM[j].astype(bf)
-
-    def own_weights(first_s, count, first_w):
-        for j in range(count):
-            r.WS[j, z, y, x] = r.SB[first_s + j]
-        for j in range(2):
-            r.WW[j, z, y, x] = r.WB[first_w + j]
-
-    pl.when(role == 0)(lambda: own_weights(0, 4, 0))
-    pl.when(role == 1)(lambda: own_weights(4, 8, 2))
-
-    loads[4].wait()
-    pl.semaphore_wait(barrier, 16)
+    def cast_weights(role_of, u):
+        kind, i, j = unit_mats(role_of, u)
+        if kind == SQUARE:
+            for m in range(4):
+                r.SB[j + m] = r.SM[j + m].astype(bf)
+
+            @pl.when(role == role_of)
+            def _():
+                for m in range(4):
+                    r.WS[4 * i + m, z, y, x] = r.SB[j + m]
+
+        else:
+            r.WB[j] = r.WM[j].astype(bf)
+
+            @pl.when(role == role_of)
+            def _():
+                r.WW[i, z, y, x] = r.WB[j]
 
     def z_slot(kind, i, k=0, yy=None, xx=None):
         zz = lax.rem(z + 4 - k, 4)
@@ -806,10 +772,6 @@
                 def _():
                     r.TREC[d] = r.TSEND[t]
 
-    def ag_own(units):
-        for u, (kind, i) in enumerate(units):
-            ag_plane(kind, i, u, 0)
-
     def ag_plane(kind, i, u, k):
         block = z_slot(kind, i, k)
         copy(block, block, (S_AX, u, k), x_mate).start()
@@ -821,10 +783,13 @@
             wait_in(z_slot(kind, i), (S_Z, u, k))
             ag_plane(kind, i, u, k)
 
-    def ag_forward(units, u):
+    def by_x(u, k):
+        return (k < 2) == (u % 2 == 0)
+
+    def ag_forward(units, u, ks=(1, 3, 2)):
         kind, i = units[u]
-        for k in (0, 1, 3, 2):
-            if k < 2:
+        for k in ks:
+            if by_x(u, k):
                 wait_in(z_slot(kind, i), (S_AY, u, k))
                 block = z_slot(kind, i, k, yy=1 - y)
                 copy(block, block, (S_FX, u, k), x_mate).start()
@@ -837,8 +802,8 @@
         kind, i = units[u]
         block = z_slot(kind, i)
         for k in (0, 1, 3, 2):
-            wait_in(block, (S_AX if k < 2 else S_AY, u, k))
-            wait_in(block, (S_FX if k < 2 else S_FY, u, k))
+            wait_in(block, (S_AX if by_x(u, k) else S_AY, u, k))
+            wait_in(block, (S_FX if by_x(u, k) else S_FY, u, k))
 
     def ag_sent(units):
         for u, (kind, i) in enumerate(units):
@@ -846,85 +811,101 @@
             for k in range(4):
                 wait_out(block, (S_AX, u, k))
                 wait_out(block, (S_AY, u, k))
-                wait_out(block, (S_FX if k < 2 else S_FY, u, k))
-
-    def rs_first(units, u):
+                wait_out(block, (S_FX if by_x(u, k) else S_FY, u, k))
+
+    def half_unit(buf, kind, i, h, *rest):
+        if kind == SQUARE:
+            return buf[0], (slice(4 * i + 2 * h, 4 * i + 2 * h + 2),) + rest
+        pad = (slice(None),) * (buf[1].ndim - 2 - len(rest))
+        return buf[1], (i,) + rest + pad + (slice(512 * h, 512 * h + 512),)
+
+    def part(buf, kind, i, h, *rest):
+        ref, index = half_unit(buf, kind, i, h, *rest)
+        return ref.at[index]
+
+    def rs_first(units, u, h):
         kind, i = units[u]
-        gref, lead = unit(G, kind, i)
+        every = slice(None)
         copy(
-            gref.at[lead + (slice(0, 2), 1 - y)], part(R1A, kind, i), (S_RA, u), y_mate
+            part(G, kind, i, h, slice(0, 2), 1 - y), part(R1A, kind, i, h), (S_RA, u, h), y_mate
         ).start()
         copy(
-            gref.at[lead + (slice(2, 4), slice(None), 1 - x)],
-            part(R1B, kind, i),
-            (S_RB, u),
+            part(G, kind, i, h, slice(2, 4), every, 1 - x),
+            part(R1B, kind, i, h),
+            (S_RB, u, h),
             x_mate,
         ).start()
 
-    def add_into(ref, index, other):
+    def add_into(place, other):
+        ref, index = place
         ref[index] = (ref[index].astype(f32) + other[...].astype(f32)).astype(bf)
 
-    def rs_second(units, u):
+    def rs_second(units, u, h):
         kind, i = units[u]
-        gref, lead = unit(G, kind, i)
-        ra, rb = part(R1A, kind, i), part(R1B, kind, i)
-        wait_in(ra, (S_RA, u))
-        add_into(gref, lead + (slice(0, 2), y), ra)
+        every = slice(None)
+        ra, rb = part(R1A, kind, i, h), part(R1B, kind, i, h)
+        wait_in(ra, (S_RA, u, h))
+        add_into(half_unit(G, kind, i, h, slice(0, 2), y), ra)
         copy(
-            gref.at[lead + (slice(0, 2), y, 1 - x)], part(R2A, kind, i), (S_SA, u), x_mate
+            part(G, kind, i, h, slice(0, 2), y, 1 - x), part(R2A, kind, i, h), (S_SA, u, h), x_mate
         ).start()
-        wait_in(rb, (S_RB, u))
-        add_into(gref, lead + (slice(2, 4), slice(None), x), rb)
+        wait_in(rb, (S_RB, u, h))
+        add_into(half_unit(G, kind, i, h, slice(2, 4), every, x), rb)
         copy(
-            gref.at[lead + (slice(2, 4), 1 - y, x)], part(R2B, kind, i), (S_SB, u), y_mate
+            part(G, kind, i, h, slice(2, 4), 1 - y, x), part(R2B, kind, i, h), (S_SB, u, h), y_mate
         ).start()
 
-    def rs_third(my_role, units, u):
+    def arrived(role_of, u, h, slot):
+        kind, i, j = unit_mats(role_of, u)
+        if kind == SQUARE:
+            return r.R3S.at[slot, j + 2 * h : j + 2 * h + 2]
+        return r.R3W.at[slot, j, :, 512 * h : 512 * h + 512]
+
+    def rs_third(my_role, u, h):
         kind, i, j = unit_mats(my_role, u)
-        gref, lead = unit(G, kind, i)
-        ra, rb = part(R2A, kind, i), part(R2B, kind, i)
-        wait_in(ra, (S_SA, u))
-        add_into(gref, lead + (slice(0, 2), y, x), ra)
-        wait_in(rb, (S_SB, u))
-        add_into(gref, lead + (slice(2, 4), y, x), rb)
-        for k in (1, 2, 3):
+        ra, rb = part(R2A, kind, i, h), part(R2B, kind, i, h)
+        wait_in(ra, (S_SA, u, h))
+        add_into(half_unit(G, kind, i, h, slice(0, 2), y, x), ra)
+        wait_in(rb, (S_SB, u, h))
+        add_into(half_unit(G, kind, i, h, slice(2, 4), y, x), rb)
+        for k in (2, 1, 3):
             slot = 1 if k == 3 else 0
             zz, dev = z_mate(k)
-            if kind == SQUARE:
-                dst = r.R3S.at[slot, j : j + 4]
-            else:
-                dst = r.R3W.at[slot, j]
-            copy(gref.at[lead + (zz, y, x)], dst, (S_T, my_role, u, slot, k & 1), dev).start()
+            copy(
+                part(G, kind, i, h, zz, y, x),
+                arrived(my_role, u, h, slot),
+                (S_T, my_role, u, h, slot, k & 1),
+                dev,
+            ).start()
 
     def rs_sent(my_role, units):
         for u, (kind, i) in enumerate(units):
-            gref, lead = unit(G, kind, i)
-            wait_out(part(R1A, kind, i), (S_RA, u))
-            wait_out(part(R1B, kind, i), (S_RB, u))
-            wait_out(part(R2A, kind, i), (S_SA, u))
-            wait_out(part(R2B, kind, i), (S_SB, u))
-            for k in (1, 2, 3):
-                slot = 1 if k == 3 else 0
-                wait_out(gref.at[lead + (0, y, x)], (S_T, my_role, u, slot, k & 1))
+            for h in range(2):
+                wait_out(part(R1A, kind, i, h), (S_RA, u, h))
+                wait_out(part(R1B, kind, i, h), (S_RB, u, h))
+                wait_out(part(R2A, kind, i, h), (S_SA, u, h))
+                wait_out(part(R2B, kind, i, h), (S_SB, u, h))
+                for k in (1, 2, 3):
+                    slot = 1 if k == 3 else 0
+                    wait_out(arrived(my_role, u, h, 0), (S_T, my_role, u, h, slot, k & 1))
 
     def final_sum(my_role, role_of, u):
         kind, i, j = unit_mats(role_of, u)
-        if kind == SQUARE:
-            dst = [r.R3S.at[slot, j : j + 4] for slot in (0, 1)]
-        else:
-            dst = [r.R3W.at[slot, j] for slot in (0, 1)]
-        if my_role == role_of:
-            wait_in(dst[0], (S_T, role_of, u, 0, 0))
-            gref, lead = unit(G, kind, i)
-            total = gref[lead + (z, y, x)].astype(f32) + dst[0][...].astype(f32)
-        else:
-            wait_in(dst[0], (S_T, role_of, u, 0, 1))
-            wait_in(dst[1], (S_T, role_of, u, 1, 1))
-            total = dst[0][...].astype(f32) + dst[1][...].astype(f32)
-        if kind == SQUARE:
-            r.F_GS[j : j + 4] = total
-        else:
-            r.F_GW[j] = total
+        for h in range(2):
+            first = arrived(role_of, u, h, 0)
+            second = arrived(role_of, u, h, 1)
+            if my_role == role_of:
+                wait_in(first, (S_T, role_of, u, h, 0, 0))
+                ref, index = half_unit(G, kind, i, h, z, y, x)
+                total = ref[index].astype(f32) + first[...].astype(f32)
+            else:
+                wait_in(first, (S_T, role_of, u, h, 0, 1))
+                wait_in(second, (S_T, role_of, u, h, 1, 1))
+                total = first[...].astype(f32) + second[...].astype(f32)
+            if kind == SQUARE:
+                r.F_GS[j + 2 * h : j + 2 * h + 2] = total
+            else:
+                r.F_GW[j, :, 512 * h : 512 * h + 512] = total
 
     def unit_stats(g):
         role_of, u = ALL_UNITS[g]
@@ -947,6 +928,11 @@
                 r.ST[g, z, h : h + 1, :] = cols[:, h * LANES : (h + 1) * LANES]
             rows = jnp.where(lanes == 12 + j, jnp.sum(sq, axis=1, keepdims=True), rows)
         r.RQ[0:32, :] = rows
+        if g == 0:
+            r.SV[d] = r.ST[0, z]
+            for k in range(1, 16):
+                copy(r.SV.at[d], r.SV.at[d], S_SV, lax.rem(d + k, 16)).start()
+            return
         for k in (1, 2, 3):
             copy(r.ST.at[g, z], r.ST.at[g, z], (S_ST, g), z_mate(k)[1]).start()
 
@@ -983,7 +969,7 @@
             rows = slice(half * BLOCK, (half + 1) * BLOCK)
             if number >= 2:
                 wait_out(r.PS.at[slot, rows], (S_M, number - 2, half))
-            r.PS[slot, rows] = partial(rows)
+            r.PS[slot, rows] = partial(rows).astype(bf)
             copy(
                 r.PS.at[slot, rows], r.PR.at[slot, rows], (S_M, number, half), d, 1 - c
             ).start()
@@ -996,7 +982,11 @@
 
             def chunk(i):
                 at = pl.ds(pl.multiple_of(half * BLOCK + i * CHUNK, CHUNK), CHUNK)
-                body(at, half * (BLOCK // CHUNK) + i, r.PS[slot, at] + r.PR[slot, at])
+                body(
+                    at,
+                    half * (BLOCK // CHUNK) + i,
+                    r.PS[slot, at].astype(f32) + r.PR[slot, at].astype(f32),
+                )
 
             repeat(BLOCK // CHUNK, chunk)
 
@@ -1104,14 +1094,8 @@
 
     def attention_back_start(kept, base):
         upstream = r.GLOW[...]
-        put_square(base + 3, mm_tn(upstream, r.O[kept]))
         r.DO[...] = mm(upstream, weight(SQUARE, base + 3)).astype(bf)
         attend_back(kept)
-
-    def attention_grads(base, queries, keys):
-        put_square(base, mm_tn(queries, r.DQ[...]))
-        put_square(base + 1, mm_tn(keys, r.DK[...]))
-        put_square(base + 2, mm_tn(keys, r.DV[...]))
 
     def query_side(base):
         return lambda rows: mm_nt(r.DQ[rows], weight(SQUARE, base))
@@ -1137,18 +1121,18 @@
     def contract(rows):
         return mm_nt(r.ACT[rows], weight(WIDE, 1))
 
-    def expand_back_down():
+    def expand_back_down(h):
         upstream = r.GLOW[...]
 
         def one(n):
-            cols = aligned(n, 256)
+            cols = aligned(2 * h + n, 256)
             r.GW[1, :, :, :, :, cols] = (
                 mm_tn(upstream, r.ACT[:, cols]).astype(bf).reshape(4, 2, 2, 32, 256)
             )
 
-        repeat(4, one)
-
-    def expand_back_up(inputs):
+        repeat(2, one)
+
+    def expand_back_hidden():
         upstream = r.GLOW[...]
 
         def one(n):
@@ -1160,13 +1144,18 @@
             slope = 0.5 * (1.0 + bent) + 0.5 * hidden * (1.0 - bent * bent) * 0.7978845608 * (
                 1.0 + 3.0 * 0.044715 * square
             )
-            hidden_grad = (active_grad * slope).astype(bf)
-            r.DU[:, cols] = hidden_grad
+            r.DU[:, cols] = (active_grad * slope).astype(bf)
+
+        repeat(4, one)
+
+    def expand_back_up(inputs, h):
+        def one(n):
+            cols = aligned(2 * h + n, 256)
             r.GW[0, :, :, :, :, cols] = (
-                mm_tn(inputs, hidden_grad).astype(bf).reshape(4, 2, 2, 32, 256)
+                mm_tn(inputs, r.DU[:, cols]).astype(bf).reshape(4, 2, 2, 32, 256)
             )
 
-        repeat(4, one)
+        repeat(2, one)
 
     def expand_input(rows):
         return mm_nt(r.DU[rows], weight(WIDE, 0))
@@ -1189,19 +1178,90 @@
                 total = total + r.NB[4 * b + i].astype(f32)
             r.NORM[:, b * LANES : (b + 1) * LANES] = total
 
+    def by_role(body):
+        pl.when(role == 0)(lambda: body(0))
+        pl.when(role == 1)(lambda: body(1))
+
+    def start_unit(u):
+        def body(my_role):
+            if u < 3:
+                z_send(my_role, 0, u)
+            units = (ENC_UNITS, DEC_UNITS)[my_role]
+            if u < len(units):
+                ag_plane(*units[u], u, 0)
+
+        by_role(body)
+
+    loads[2].wait()
+    cast_weights(0, 0)
+    cast_weights(1, 0)
+    pl.semaphore_wait(barrier, 16)
+    start_unit(0)
+    loads[3].wait()
+    cast_weights(0, 1)
+    cast_weights(1, 1)
+    start_unit(1)
+    cast_weights(0, 2)
+    cast_weights(1, 2)
+    start_unit(2)
+    cast_weights(1, 3)
+    start_unit(3)
+
+    r.NORM[...] = jnp.zeros((16, 512), f32)
+    r.NORM[0:10, 0:32] = r.norm[...]
+    shift = lax.rem(d, 4) * 32
+    r.NB[d] = pltpu.roll(r.NORM[:, 0:LANES], shift, 1).astype(bf)
+    r.RL[...] = jnp.zeros((16, LANES), f32)
+    r.RL[0:12, 0:32] = r.square_rows[...]
+    r.RL[12:16, 0:32] = r.wide_rows[...]
+
+    send_norms()
+
+    lane = lax.broadcasted_iota(jnp.int32, (8, LANES), 1)
+    for s in range(16):
+        r.EXT[8 * s : 8 * s + 8, :] = jnp.where(
+            lane < 32,
+            r.lengths[0, s],
+            jnp.where(lane < 64, r.lengths[1, s], r.destinations[s]),
+        ).astype(f32)
+    ext_low = r.EXT[...].astype(bf)
+    r.SEXT[...] = ext_low
+
+    loads[1].wait()
+
+    @pl.when(role == 1)
+    def _():
+        copy(r.SRC.at[:, my_half], r.XHALF.at[c], S_SOURCE, partner).start()
+        copy(r.SEXT, r.XEXT, S_EXT, partner).start()
+
+    def later_units(my_role, us):
+        for u in us:
+            z_send(my_role, 1, u)
+
+    by_role(lambda my_role: later_units(my_role, (0, 1)))
+
+    perm_f = perm_of(r.EXT[:, 64:65])
+    r.PERMT[0] = perm_f.astype(bf)
+    perm = perm_f.T.astype(bf)
+    loads[0].wait()
+    r.TSEND[:, :, 0:512] = mm(perm, r.TGT[...]).astype(bf).reshape(8, 16, 512)
+    r.TSEND[:, :, 512:640] = mm(perm, ext_low).astype(bf).reshape(8, 16, LANES)
+
+    loads[4].wait()
+
+    def last_starts(my_role):
+        send_target(my_role)
+        later_units(my_role, (2, 3))
+        if my_role == 0:
+            copy(r.COT1, r.COT2, S_COT, partner).start()
+
+    by_role(last_starts)
+
     def encoder():
         units = ENC_UNITS
+        clear_sums()
         for u in range(3):
-            z_send(0, 0, u)
-        ag_own(units)
-        send_norms()
-        z_send(0, 1, 0)
-        z_send(0, 1, 1)
-        send_target(0)
-        z_send(0, 1, 2)
-        z_send(0, 1, 3)
-        copy(r.COT1, r.COT2, S_COT, partner).start()
-        clear_sums()
+            ag_forward(units, u, (0,))
         ag_column(units, 0)
         ag_forward(units, 0)
         ag_column(units, 1)
@@ -1269,11 +1329,14 @@
             r.GLOW[at] = value.astype(bf)
 
         repeat(TOKENS // CHUNK, back_one)
-        expand_back_down()
-        rs_first(units, 2)
-        expand_back_up(r.LOW[0])
-        rs_first(units, 1)
+        for h in range(2):
+            expand_back_down(h)
+            rs_first(units, 2, h)
+        expand_back_hidden()
         swap(2, expand_input)
+        for h in range(2):
+            expand_back_up(r.LOW[0], h)
+            rs_first(units, 1, h)
 
         def back_two(at, n, total):
             value = norm_backward(r.GRAD[at] + total, 0, 0, at)
@@ -1282,10 +1345,15 @@
 
         swapped(2, back_two)
         attention_back_start(0, 0)
-        attention_grads(0, r.XT[...], r.XT[...])
-        rs_first(units, 0)
+        put_square(3, mm_tn(r.GLOW[...], r.O[0]))
+        put_square(2, mm_tn(r.XT[...], r.DV[...]))
+        rs_first(units, 0, 1)
+        put_square(0, mm_tn(r.XT[...], r.DQ[...]))
+        put_square(1, mm_tn(r.XT[...], r.DK[...]))
+        rs_first(units, 0, 0)
+        rs_second(units, 2, 0)
+        rs_second(units, 2, 1)
         swap(3, all_sides(0))
-        rs_second(units, 2)
 
         def back_three(at, n, total):
             r.GRAD[at] = r.GRAD[at] + total
@@ -1298,16 +1366,21 @@
         copy(r.SGSEND, r.SGREC, S_SG, partner).start()
         send_norm_sums()
         finish_unit(0, 6)
+        rs_second(units, 1, 0)
+        rs_second(units, 1, 1)
+        rs_third(0, 2, 0)
+        rs_third(0, 2, 1)
         take_target(0)
-        rs_second(units, 1)
-        rs_third(0, units, 2)
         finish_unit(0, 5)
-        rs_second(units, 0)
+        rs_second(units, 0, 1)
+        rs_second(units, 0, 0)
+        rs_third(0, 1, 0)
+        rs_third(0, 1, 1)
         finish_unit(0, 4)
-        rs_third(0, units, 1)
         finish_unit(0, 2)
+        rs_third(0, 0, 1)
+        rs_third(0, 0, 0)
         finish_unit(0, 3)
-        rs_third(0, units, 0)
         wait_out(r.MREC.at[0], S_MEMORY)
         wait_out(r.SGSEND, S_SG)
         swaps_sent(4)
@@ -1319,7 +1392,6 @@
         spread_unit(3)
         finish_unit(0, 0)
         spread_unit(1)
-        spread_unit(0)
         ag_sent(units)
         rs_sent(0, units)
         z_sent(0)
@@ -1353,19 +1425,9 @@
 
     def decoder():
         units = DEC_UNITS
-        z_send(1, 0, 0)
-        copy(r.SRC.at[:, my_half], r.XHALF.at[c], S_SOURCE, partner).start()
-        copy(r.SEXT, r.XEXT, S_EXT, partner).start()
-        z_send(1, 0, 1)
-        z_send(1, 0, 2)
-        ag_own(units)
-        send_norms()
-        for u in range(2):
-            z_send(1, 1, u)
-        send_target(1)
-        for u in range(2, 4):
-            z_send(1, 1, u)
         clear_sums()
+        for u in range(4):
+            ag_forward(units, u, (0,))
         ag_column(units, 0)
         ag_forward(units, 0)
         ag_column(units, 1)
@@ -1448,13 +1510,13 @@
             r.GLOW[at] = value.astype(bf)
 
         swapped(2, third)
-        expand_back_down()
-        rs_first(units, 3)
+        expand_back_hidden()
+        swap(3, expand_input)
+        for h in range(2):
+            expand_back_down(h)
+            rs_first(units, 3, h)
         copy(r.DSEND, r.DREC, S_DEC, partner).start()
         local(r.F_DEC, r.o_dec, 5).start()
-        expand_back_up(r.LOW[1])
-        rs_first(units, 2)
-        swap(3, expand_input)
 
         def back_two(at, n, total):
             value = norm_backward(r.GRAD[at] + total, 1, 3, at)
@@ -1464,7 +1526,8 @@
         swapped(3, back_two)
         attention_back_start(1, 4)
         swap(4, key_side(4))
-        attention_grads(4, r.LOW[0], r.MEM[...])
+        for h in range(2):
+            expand_back_up(r.LOW[1], h)
 
         def back_memory(at, n, total):
             r.LOW[2, at] = total.astype(bf)
@@ -1477,9 +1540,16 @@
             copy(
                 r.DMSEND.at[t // 4, :, t % 4, :, my_half], r.MG.at[c, my_t], S_DM, dev
             ).start()
-        rs_first(units, 1)
+        for h in range(2):
+            rs_second(units, 3, h)
+            rs_first(units, 2, h)
         swap(5, query_side(4))
-        rs_second(units, 3)
+        put_square(7, mm_tn(r.GLOW[...], r.O[1]))
+        put_square(6, mm_tn(r.MEM[...], r.DV[...]))
+        rs_first(units, 1, 1)
+        put_square(5, mm_tn(r.MEM[...], r.DK[...]))
+        put_square(4, mm_tn(r.LOW[0], r.DQ[...]))
+        rs_first(units, 1, 0)
 
         def back_three(at, n, total):
             value = norm_backward(r.GRAD[at] + total, 0, 2, at)
@@ -1488,10 +1558,17 @@
 
         swapped(5, back_three)
         attention_back_start(0, 0)
-        attention_grads(0, r.XT[...], r.XT[...])
-        rs_first(units, 0)
         swap(6, all_sides(0))
-        rs_second(units, 2)
+        put_square(3, mm_tn(r.GLOW[...], r.O[0]))
+        put_square(2, mm_tn(r.XT[...], r.DV[...]))
+        rs_first(units, 0, 1)
+        put_square(0, mm_tn(r.XT[...], r.DQ[...]))
+        put_square(1, mm_tn(r.XT[...], r.DK[...]))
+        rs_third(1, 3, 0)
+        rs_third(1, 3, 1)
+        rs_second(units, 2, 0)
+        rs_second(units, 2, 1)
+        rs_first(units, 0, 0)
 
         def back_four(at, n, total):
             r.DTSEND[aligned(n, 4)] = (
@@ -1504,15 +1581,19 @@
             copy(r.DTSEND.at[dev, :, my_half], r.TG.at[c, my_t], S_DT, dev).start()
         r.TG[c, my_t] = r.DTSEND[d, :, my_half]
         send_norm_sums()
-        rs_third(1, units, 3)
-        rs_second(units, 1)
-        rs_third(1, units, 2)
+        rs_second(units, 1, 1)
+        rs_third(1, 2, 0)
+        rs_second(units, 1, 0)
+        rs_third(1, 2, 1)
         finish_unit(1, 6)
-        rs_second(units, 0)
-        rs_third(1, units, 1)
+        rs_second(units, 0, 1)
+        rs_third(1, 1, 1)
+        rs_second(units, 0, 0)
+        rs_third(1, 1, 0)
         finish_unit(1, 5)
         take_target(1)
-        rs_third(1, units, 0)
+        rs_third(1, 0, 1)
+        rs_third(1, 0, 0)
         finish_unit(1, 4)
         finish_unit(1, 2)
         wait_in(r.SGREC, S_SG)
@@ -1531,7 +1612,6 @@
         spread_unit(3)
         finish_unit(1, 0)
         spread_unit(1)
-        spread_unit(0)
         ag_sent(units)
         rs_sent(1, units)
         z_sent(1)
@@ -1549,8 +1629,14 @@
     r.o_ng[...] = pltpu.roll(total, lax.rem(LANES - shift, LANES), 1)
     r.o_rl[...] = total
     for g in (6, 5, 4, 2, 3, 1, 0):
-        wait_in(r.SU.at[g, 0:3], (S_SU, g))
-        total = in_order(r.SU, (g,))
+        if g == 0:
+            wait_in(r.SV.at[0:15], S_SV)
+            total = r.SV[0]
+            for i in range(1, 16):
+                total = total + r.SV[i]
+        else:
+            wait_in(r.SU.at[g, 0:3], (S_SU, g))
+            total = in_order(r.SU, (g,))
         r.TT[g] = jnp.broadcast_to(jnp.sum(total, axis=1, keepdims=True), (8, LANES))
         role_of, u = ALL_UNITS[g]
         kind, _, j = unit_mats(role_of, u)
@@ -1568,7 +1654,8 @@
     wait_out(r.TT, S_TT)
     wait_out(r.NG.at[0:3], S_NG)
     wait_out(r.NH.at[0:3], S_NH)
-    for g in range(7):
+    wait_out(r.SV.at[0:15], S_SV)
+    for g in range(1, 7):
         wait_out(r.ST.at[g, 0:3], (S_ST, g))
         wait_out(r.SU.at[g, 0:3], (S_SU, g))
     local(r.F_DEC, r.o_dec, 5).wait()

time: 134 us -> 125 us (0.933)
  Pallas kernels: 133 us -> 124 us
    pallas_call x1, Pallas kernels: 129 us -> 120 us  [small_shards(): pl.pallas_call(exchange_kernel, out_shape=[jax.ShapeDtypeStruct(*v) for v...]
where the time goes in v3:
time: 125 us; the launch traced here: 124 us
  Pallas kernels  124 us (99%)
    pallas_call x1, Pallas kernels, small_shards(): pl.pallas_call(exchange_kernel, out_shape=[jax.ShapeDtypeStruct(*v) for v...  120 us
    pallas_call x1, Pallas kernels, small_shards(): pl.pallas_call(update_kernel, out_shape=[jax.ShapeDtypeStruct(*v) for v i...  3.78 us

profile of v3, /device:TPU:0, one launch (start us, length us, event | category | flops | bytes accessed | tf_op | source)
XLA Modules:
  0.0 124.4 jit_solution(13886996344638964141)
XLA Ops:
  0.7 119.7 %shard_map.260 = (bf16[128,512]{1,0:T(8,128)(2,1)}, f32[16,4,512]{2,1,0:T(4,128)}, f32[128,512]{1,0:T(8,128)}, f32[12,32,256]{2,1,0:T(8,128)}, f32[4,32,1024]{2,...) custom-call(s32[2,16]{1,0:T(2,128)} %bitcast.7, ...), custom_call_target="tpu_custom_call" | custom-call | tf_op jit(solution)/shard_map/pallas_call | solution.py:1789
  120.4 3.8 %shard_map.261 = (bf16[16,4,512]{2,1,0:T(4,128)(2,1)}, f32[16,4,512]{2,1,0:T(4,128)}, f32[16,8,512]{2,1,0:T(8,128)}, f32[12,32,256]{2,1,0:T(8,128)}, f32[12,32]{...) custom-call(bf16[128,512]{1,0:T(8,128)(2,1)} %get-tuple-element.28.r, ...), custom_call_target="tpu_custom_call" | custom-call | tf_op jit(solution)/shard_map/pallas_call | solution.py:1812

commit v4 on v3

--- a/solution.py
+++ b/solution.py
@@ -483,7 +483,7 @@
 
 
 SEM_COUNT = 240
-NEAR_COUNT = 16
+NEAR_COUNT = 18
 (
     S_AX,
     S_AY,
@@ -595,10 +595,13 @@
     WM=((4, 32, 1024), jnp.float32),
     SRC=((BLOCK, 512), jnp.bfloat16),
     TGT=((BLOCK, 512), jnp.bfloat16),
+    I_NORM=((10, 32), jnp.float32),
+    I_SR=((12, 32), jnp.float32),
+    I_WR=((4, 32), jnp.float32),
     COT1=((BLOCK, 512), jnp.bfloat16),
     F_DEC=((BLOCK, 512), jnp.bfloat16),
     F_SRC=((16, 4, 512), jnp.float32),
-    F_TGT=((BLOCK, 512), jnp.float32),
+    F_TGT=((16, 8, 512), jnp.float32),
     F_GS=((12, 32, 256), jnp.float32),
     F_GW=((4, 32, 1024), jnp.float32),
     TTR=((7, 8, LANES), jnp.float32),
@@ -619,7 +622,7 @@
 OUTPUTS = dict(
     o_dec=((BLOCK, 512), jnp.bfloat16),
     o_src=((16, 4, 512), jnp.float32),
-    o_tgt=((BLOCK, 512), jnp.float32),
+    o_tgt=((16, 8, 512), jnp.float32),
     o_gs=((12, 32, 256), jnp.float32),
     o_gw=((4, 32, 1024), jnp.float32),
     o_cs=((12, 256), jnp.float32),
@@ -697,8 +700,11 @@
         local(r.square, r.SM, 2),
         local(r.wide, r.WM, 3),
         local(r.cotangent, r.COT1, 4),
+        local(r.norm, r.I_NORM, 15),
+        local(r.square_rows, r.I_SR, 16),
+        local(r.wide_rows, r.I_WR, 17),
     ]
-    for i in (2, 3, 1, 0, 4):
+    for i in (2, 3, 5, 6, 7, 1, 0, 4):
         loads[i].start()
     barrier = pltpu.get_barrier_semaphore()
     for k in range(1, 16):
@@ -1208,12 +1214,14 @@
     start_unit(3)
 
     r.NORM[...] = jnp.zeros((16, 512), f32)
-    r.NORM[0:10, 0:32] = r.norm[...]
+    for i in (5, 6, 7):
+        loads[i].wait()
+    r.NORM[0:10, 0:32] = r.I_NORM[...]
     shift = lax.rem(d, 4) * 32
     r.NB[d] = pltpu.roll(r.NORM[:, 0:LANES], shift, 1).astype(bf)
     r.RL[...] = jnp.zeros((16, LANES), f32)
-    r.RL[0:12, 0:32] = r.square_rows[...]
-    r.RL[12:16, 0:32] = r.wide_rows[...]
+    r.RL[0:12, 0:32] = r.I_SR[...]
+    r.RL[12:16, 0:32] = r.I_WR[...]
 
     send_norms()
 
@@ -1311,9 +1319,6 @@
                 r.MSEND.at[t, :, :, my_half], r.MREC.at[c, zz, :, yx], S_MEMORY, dev
             ).start()
 
-        wait_in(r.DREC, S_DEC)
-        r.F_DEC[...] = r.DREC[...]
-        local(r.F_DEC, r.o_dec, 5).start()
         wait_in(r.MG.at[0], S_DM)
         hand_over(r.MG, S_DM2)
         for jj in range(2):
@@ -1344,16 +1349,15 @@
             r.GLOW[at] = value.astype(bf)
 
         swapped(2, back_two)
+        rs_second(units, 2, 0)
         attention_back_start(0, 0)
+        swap(3, all_sides(0))
+        rs_second(units, 2, 1)
         put_square(3, mm_tn(r.GLOW[...], r.O[0]))
         put_square(2, mm_tn(r.XT[...], r.DV[...]))
         rs_first(units, 0, 1)
         put_square(0, mm_tn(r.XT[...], r.DQ[...]))
         put_square(1, mm_tn(r.XT[...], r.DK[...]))
-        rs_first(units, 0, 0)
-        rs_second(units, 2, 0)
-        rs_second(units, 2, 1)
-        swap(3, all_sides(0))
 
         def back_three(at, n, total):
             r.GRAD[at] = r.GRAD[at] + total
@@ -1365,11 +1369,15 @@
         local(r.F_SRC, r.o_src, 6).start()
         copy(r.SGSEND, r.SGREC, S_SG, partner).start()
         send_norm_sums()
-        finish_unit(0, 6)
+        rs_first(units, 0, 0)
         rs_second(units, 1, 0)
         rs_second(units, 1, 1)
         rs_third(0, 2, 0)
         rs_third(0, 2, 1)
+        finish_unit(0, 6)
+        wait_in(r.DREC, S_DEC)
+        r.F_DEC[...] = r.DREC[...]
+        local(r.F_DEC, r.o_dec, 5).start()
         take_target(0)
         finish_unit(0, 5)
         rs_second(units, 0, 1)
@@ -1418,9 +1426,9 @@
             wait_in(r.TG.at[0, 0:7], S_DT)
         hand_over(r.TG, S_DT2)
         for half in range(2):
-            r.F_TGT[:, half * 256 : half * 256 + 256] = mm(
+            r.F_TGT[:, :, half * 256 : half * 256 + 256] = mm(
                 r.PERMT[0], r.TG[half].reshape(BLOCK, 256)
-            )
+            ).reshape(16, 8, 256)
         local(r.F_TGT, r.o_tgt, 7).start()
 
     def decoder():
@@ -1515,7 +1523,6 @@
         for h in range(2):
             expand_back_down(h)
             rs_first(units, 3, h)
-        copy(r.DSEND, r.DREC, S_DEC, partner).start()
         local(r.F_DEC, r.o_dec, 5).start()
 
         def back_two(at, n, total):
@@ -1540,6 +1547,7 @@
             copy(
                 r.DMSEND.at[t // 4, :, t % 4, :, my_half], r.MG.at[c, my_t], S_DM, dev
             ).start()
+        copy(r.DSEND, r.DREC, S_DEC, partner).start()
         for h in range(2):
             rs_second(units, 3, h)
             rs_first(units, 2, h)
@@ -1707,7 +1715,7 @@
 
     r.decoded[...] = own_half(r.o_dec[...]).astype(bf)
     r.source_grad[...] = r.o_src[...]
-    r.target_grad[...] = r.o_tgt[...].reshape(16, 8, 512)
+    r.target_grad[...] = r.o_tgt[...]
     pad = r.rows_pad
     pad[...] = jnp.zeros((BLOCK, LANES), f32)
     pad[0:12, 0:32] = r.square_rows[...]
@@ -1789,7 +1797,7 @@
     moved = pl.pallas_call(
         exchange_kernel,
         out_shape=[jax.ShapeDtypeStruct(*v) for v in OUTPUTS.values()],
-        in_specs=[smem, smem] + [anywhere] * 5 + [vmem] * 3,
+        in_specs=[smem, smem] + [anywhere] * 5 + [anywhere] * 3,
         out_specs=[anywhere] * 5 + [vmem] * (len(OUTPUTS) - 5),
         scratch_shapes=[pltpu.VMEM(*v) for v in SCRATCH.values()]
         + [pltpu.SemaphoreType.DMA((n,)) for n in (SEM_COUNT, SEM_COUNT, NEAR_COUNT)],

time: 125 us -> 123 us (0.984)
  Pallas kernels: 124 us -> 121 us
    pallas_call x1, Pallas kernels: 120 us -> 118 us  [small_shards(): pl.pallas_call(exchange_kernel, out_shape=[jax.ShapeDtypeStruct(*v) for v...]
where the time goes in v4:
time: 123 us; the launch traced here: 122 us
  Pallas kernels  121 us (98%)
    pallas_call x1, Pallas kernels, small_shards(): pl.pallas_call(exchange_kernel, out_shape=[jax.ShapeDtypeStruct(*v) for v...  118 us
    pallas_call x1, Pallas kernels, small_shards(): pl.pallas_call(update_kernel, out_shape=[jax.ShapeDtypeStruct(*v) for v i...  3.78 us

profile of v4, /device:TPU:0, one launch (start us, length us, event | category | flops | bytes accessed | tf_op | source)
XLA Modules:
  0.0 122.3 jit_solution(15080800118565578409)
XLA Ops:
  0.7 117.7 %shard_map.260 = (bf16[128,512]{1,0:T(8,128)(2,1)}, f32[16,4,512]{2,1,0:T(4,128)}, f32[16,8,512]{2,1,0:T(8,128)}, f32[12,32,256]{2,1,0:T(8,128)}, f32[4,32,1024]...) custom-call(s32[2,16]{1,0:T(2,128)} %bitcast.7, ...), custom_call_target="tpu_custom_call" | custom-call | tf_op jit(solution)/shard_map/pallas_call | solution.py:1797
  118.4 3.8 %shard_map.261 = (bf16[16,4,512]{2,1,0:T(4,128)(2,1)}, f32[16,4,512]{2,1,0:T(4,128)}, f32[16,8,512]{2,1,0:T(8,128)}, f32[12,32,256]{2,1,0:T(8,128)}, f32[12,32]{...) custom-call(bf16[128,512]{1,0:T(8,128)(2,1)} %get-tuple-element.28.r, ...), custom_call_target="tpu_custom_call" | custom-call | tf_op jit(solution)/shard_map/pallas_call | solution.py:1820

commit v5 on v4

--- a/solution.py
+++ b/solution.py
@@ -1198,6 +1198,10 @@
 
         by_role(body)
 
+    def later_units(my_role, us):
+        for u in us:
+            z_send(my_role, 1, u)
+
     loads[2].wait()
     cast_weights(0, 0)
     cast_weights(1, 0)
@@ -1207,6 +1211,7 @@
     cast_weights(0, 1)
     cast_weights(1, 1)
     start_unit(1)
+    by_role(lambda my_role: later_units(my_role, (0,)))
     cast_weights(0, 2)
     cast_weights(1, 2)
     start_unit(2)
@@ -1242,11 +1247,7 @@
         copy(r.SRC.at[:, my_half], r.XHALF.at[c], S_SOURCE, partner).start()
         copy(r.SEXT, r.XEXT, S_EXT, partner).start()
 
-    def later_units(my_role, us):
-        for u in us:
-            z_send(my_role, 1, u)
-
-    by_role(lambda my_role: later_units(my_role, (0, 1)))
+    by_role(lambda my_role: later_units(my_role, (1,)))
 
     perm_f = perm_of(r.EXT[:, 64:65])
     r.PERMT[0] = perm_f.astype(bf)

time: 123 us -> 121 us (0.984)
    pallas_call x1, Pallas kernels: 118 us -> 116 us  [small_shards(): pl.pallas_call(exchange_kernel, out_shape=[jax.ShapeDtypeStruct(*v) for v...]
where the time goes in v5:
time: 121 us
  Pallas kernels  120 us (99%)
    pallas_call x1, Pallas kernels, small_shards(): pl.pallas_call(exchange_kernel, out_shape=[jax.ShapeDtypeStruct(*v) for v...  116 us
    pallas_call x1, Pallas kernels, small_shards(): pl.pallas_call(update_kernel, out_shape=[jax.ShapeDtypeStruct(*v) for v i...  3.78 us

profile of v5, /device:TPU:0, one launch (start us, length us, event | category | flops | bytes accessed | tf_op | source)
XLA Modules:
  0.0 120.6 jit_solution(4479795975157786892)
XLA Ops:
  0.7 115.9 %shard_map.260 = (bf16[128,512]{1,0:T(8,128)(2,1)}, f32[16,4,512]{2,1,0:T(4,128)}, f32[16,8,512]{2,1,0:T(8,128)}, f32[12,32,256]{2,1,0:T(8,128)}, f32[4,32,1024]...) custom-call(s32[2,16]{1,0:T(2,128)} %bitcast.7, ...), custom_call_target="tpu_custom_call" | custom-call | tf_op jit(solution)/shard_map/pallas_call | solution.py:1798
  116.6 3.8 %shard_map.261 = (bf16[16,4,512]{2,1,0:T(4,128)(2,1)}, f32[16,4,512]{2,1,0:T(4,128)}, f32[16,8,512]{2,1,0:T(8,128)}, f32[12,32,256]{2,1,0:T(8,128)}, f32[12,32]{...) custom-call(bf16[128,512]{1,0:T(8,128)(2,1)} %get-tuple-element.28.r, ...), custom_call_target="tpu_custom_call" | custom-call | tf_op jit(solution)/shard_map/pallas_call | solution.py:1821
